TPU v7x, 32 devices: a whole 2x2x4 slice. The times are simulated.
32 devices in a mesh: dp: 16 (over z, y, core), tensor: 2 (over x).
Axes of the slice: x: 2, y: 2, z: 4, core: 2. Of those that a mesh axis runs over, the one named last changes fastest.
Arguments:
- inputs: bfloat16 [2, 16384, 768], P(None, ('dp', 'tensor')), may hold values from -6 to 6
- segments: int32 [2, 16, 1024], P(None, 'dp'), may hold values from 0 to 15, never falling along the last dimension, each value on 1 to 512 neighbouring positions
- norm_attn: float32 [768], replicated, may hold values from 0.25 to 1.75
- norm_ffn: float32 [768], replicated, may hold values from 0.25 to 1.75
- w_query: bfloat16 [768, 768], P('dp', 'tensor'), may hold values from -0.02734375 to 0.02734375
- w_key: bfloat16 [768, 768], P('dp', 'tensor'), may hold values from -0.21875 to 0.21875
- w_value: bfloat16 [768, 768], P('dp', 'tensor'), may hold values from -0.21875 to 0.21875
- w_out: bfloat16 [768, 768], P('dp', 'tensor'), may hold values from -1.75 to 1.75
- w_in: bfloat16 [768, 3072], P('dp', 'tensor'), may hold values from -0.21875 to 0.21875
- w_back: bfloat16 [768, 3072], P('dp', 'tensor'), may hold values from -0.109375 to 0.109375
- rel_table: float32 [32, 12], P(None, 'tensor'), may hold values from -4 to 4
- cotangent: float32 [2, 16384, 768], P(None, ('dp', 'tensor')), may hold values from -6 to 6
Outputs:
- output: float32 [2, 16384, 768], P(None, ('dp', 'tensor'))
- input_grad: float32 [2, 16384, 768], P(None, ('dp', 'tensor'))
- grad_norm_attn: float32 [768], replicated
- grad_norm_ffn: float32 [768], replicated
- grad_w_query: float32 [768, 768], P('dp', 'tensor')
- grad_w_key: float32 [768, 768], P('dp', 'tensor')
- grad_w_value: float32 [768, 768], P('dp', 'tensor')
- grad_w_out: float32 [768, 768], P('dp', 'tensor')
- grad_w_in: float32 [768, 3072], P('dp', 'tensor')
- grad_w_back: float32 [768, 3072], P('dp', 'tensor')
- grad_rel_table: float32 [32, 12], P(None, 'tensor')
Inputs may be any that keep to these rules, and one draw needn't show every extreme that they name: `segments`: within each sequence of 1024 tokens the segment numbers never fall, every segment has 1 to 512 tokens, and some segment has exactly 512.
All inputs are finite; a program needn't handle non-finite values.
Results may differ from a plain program's by a relative error of at most 0.014.
Values may be sent and summed in bfloat16 or wider, within the bound.
A program may use at most 384 MiB of HBM per device.

v0:
```python
import jax
import jax.numpy as jnp
from jax import lax
from jax.sharding import PartitionSpec as P

DH = 64


HIGHEST = lax.Precision.HIGHEST
EPSILON = 1e-06
MASKED = -1000000000.0
THRESHOLDS = (12, 16, 23, 32, 46, 64, 91)


def smooth_act(values):
    return (
        0.5
        * values
        * (1.0 + jnp.tanh(0.7978845608028654 * (values + 0.044715 * values * values * values)))
    )


def bucket_ids(offsets):
    distance = jnp.abs(offsets)
    far_ids = 8 + sum(((distance >= threshold).astype(jnp.int32) for threshold in THRESHOLDS))
    return jnp.where(offsets > 0, 16, 0).astype(jnp.int32) + jnp.where(
        distance < 8, distance, far_ids
    )


def matmul(left, right):
    return jnp.dot(left, right, preferred_element_type=jnp.float32)


def matmul_nt(left, right):
    return lax.dot_general(
        left, right, (((1,), (1,)), ((), ())), preferred_element_type=jnp.float32
    )


def matmul_tn(left, right):
    return lax.dot_general(
        left, right, (((0,), (0,)), ((), ())), preferred_element_type=jnp.float32
    )


def rms_scale(values):
    return lax.rsqrt(jnp.mean(values * values, -1, keepdims=True) + EPSILON)


def rms_back(grad_normed, normed, scale, gain):
    scaled = grad_normed * gain
    return scale * (scaled - normed * jnp.mean(scaled * normed, -1, keepdims=True))


def toeplitz_rows(vector, length):
    padded = jnp.concatenate([vector, jnp.zeros((1,), vector.dtype)])
    flattened = jnp.broadcast_to(padded, (length, 2 * length)).reshape(-1)
    window = lax.slice_in_dim(flattened, length - 1, length - 1 + length * (2 * length - 1))
    return window.reshape(length, 2 * length - 1)[:, :length]


def diagonal_sums(matrix, length):
    widened = jnp.pad(matrix, ((0, 0), (0, length - 1))).reshape(-1)
    placed = jnp.pad(widened, (length - 1, 1)).reshape(length, 2 * length)
    return jnp.sum(placed, 0)[: 2 * length - 1]


def bias_planes(bias_source, onehot, length):
    per_offset = jnp.dot(onehot, bias_source, precision=HIGHEST)
    return lax.map(lambda column: toeplitz_rows(column, length), per_offset.T)


def bias_table(bias_sums, onehot, length):
    diagonals = lax.map(lambda matrix: diagonal_sums(matrix, length), bias_sums)
    return jnp.dot(onehot.T, diagonals.T, precision=HIGHEST)


def masked_scores(queries, key_rows, rel_bias, segment_row):
    scores = (
        jnp.einsum("qhe,khe->hqk", queries, key_rows, preferred_element_type=jnp.float32) + rel_bias
    )
    same_doc = segment_row[:, None] == segment_row[None, :]
    return jnp.where(same_doc[None], scores, MASKED)


def attend(queries, key_rows, value_rows, rel_bias, segment_row):
    scores = masked_scores(queries, key_rows, rel_bias, segment_row)
    highest = jnp.max(scores, -1, keepdims=True)
    logsum = highest + jnp.log(jnp.sum(jnp.exp(scores - highest), -1, keepdims=True))
    attn_probs = jnp.exp(scores - logsum).astype(jnp.bfloat16)
    context = jnp.einsum("hqk,khe->qhe", attn_probs, value_rows, preferred_element_type=jnp.float32)
    return (context.astype(jnp.bfloat16), logsum)


def attend_back(queries, key_rows, value_rows, grad_context, rel_bias, segment_row, logsum):
    scores = masked_scores(queries, key_rows, rel_bias, segment_row)
    attn_probs = jnp.exp(scores - logsum)
    grad_probs = jnp.einsum(
        "qhe,khe->hqk", grad_context, value_rows, preferred_element_type=jnp.float32
    )
    totals = jnp.sum(attn_probs * grad_probs, -1, keepdims=True)
    score_grad = (attn_probs * (grad_probs - totals)).astype(jnp.bfloat16)
    query_grad = jnp.einsum(
        "hqk,khe->qhe", score_grad, key_rows, preferred_element_type=jnp.float32
    ).astype(jnp.bfloat16)
    key_grad = jnp.einsum(
        "hqk,qhe->khe", score_grad, queries, preferred_element_type=jnp.float32
    ).astype(jnp.bfloat16)
    value_grad = jnp.einsum(
        "hqk,qhe->khe",
        attn_probs.astype(jnp.bfloat16),
        grad_context,
        preferred_element_type=jnp.float32,
    ).astype(jnp.bfloat16)
    return (query_grad, key_grad, value_grad, score_grad.astype(jnp.float32))


def one_micro(rows_in, grad_top, segment_now, fetch_weights, rel_bias, norm_attn, norm_ffn):
    seq_count, length = segment_now.shape
    full_query, full_key, full_value, full_out, full_in, full_back = fetch_weights()
    inner_width = full_query.shape[1]
    shaped = (seq_count, length, inner_width // DH, DH)
    scale_attn = rms_scale(rows_in)
    normed_attn = rows_in * scale_attn
    attn_low = (normed_attn * norm_attn).astype(jnp.bfloat16)
    cot_low = grad_top.astype(jnp.bfloat16)
    seq_attn, seq_grad_ffn = (
        lax.all_gather(attn_low, "tensor", axis=0, tiled=True),
        lax.all_gather(cot_low, "tensor", axis=0, tiled=True),
    )
    queries = matmul(seq_attn, full_query).astype(jnp.bfloat16).reshape(shaped)
    key_rows = matmul(seq_attn, full_key).astype(jnp.bfloat16).reshape(shaped)
    value_rows = matmul(seq_attn, full_value).astype(jnp.bfloat16).reshape(shaped)

    def forward_one(packed):
        return attend(packed[0], packed[1], packed[2], rel_bias, packed[3])

    context, logsum = lax.map(forward_one, (queries, key_rows, value_rows, segment_now))
    context = context.reshape(seq_count * length, inner_width)
    attended = matmul_nt(context, full_out)
    attended = lax.psum_scatter(attended, "tensor", scatter_dimension=0, tiled=True)
    middle = rows_in + attended
    scale_ffn = rms_scale(middle)
    normed_ffn = middle * scale_ffn
    ffn_low = (normed_ffn * norm_ffn).astype(jnp.bfloat16)
    seq_ffn = lax.all_gather(ffn_low, "tensor", axis=0, tiled=True)
    pre_act = matmul(seq_ffn, full_in)
    activated, act_pull = jax.vjp(smooth_act, pre_act)
    hidden = activated.astype(jnp.bfloat16)
    ffn_out = matmul_nt(hidden, full_back)
    ffn_out = lax.psum_scatter(
        ffn_out.astype(jnp.bfloat16), "tensor", scatter_dimension=0, tiled=True
    ).astype(jnp.float32)
    output = middle + ffn_out
    full_query, full_key, full_value, full_out, full_in, full_back = fetch_weights()
    grad_back = matmul_tn(seq_grad_ffn, hidden)
    grad_hidden = matmul(seq_grad_ffn, full_back)
    grad_pre = act_pull(grad_hidden)[0].astype(jnp.bfloat16)
    grad_in = matmul_tn(seq_ffn, grad_pre)
    grad_normed_ffn = matmul_nt(grad_pre, full_in)
    grad_normed_ffn = lax.psum_scatter(
        grad_normed_ffn.astype(jnp.bfloat16), "tensor", scatter_dimension=0, tiled=True
    ).astype(jnp.float32)
    gain_ffn_term = jnp.sum(grad_normed_ffn * normed_ffn, 0)
    grad_middle = grad_top + rms_back(grad_normed_ffn, normed_ffn, scale_ffn, norm_ffn)
    cot_attn = grad_middle.astype(jnp.bfloat16)
    seq_grad_attn = lax.all_gather(cot_attn, "tensor", axis=0, tiled=True)
    grad_out = matmul_tn(seq_grad_attn, context)
    grad_context = matmul(seq_grad_attn, full_out).astype(jnp.bfloat16).reshape(shaped)

    def backward_one(carry, packed):
        query_grad, key_grad, value_grad, score_grad = attend_back(
            packed[0], packed[1], packed[2], packed[3], rel_bias, packed[4], packed[5]
        )
        return (carry + score_grad, (query_grad, key_grad, value_grad))

    bias_sums, grads_qkv = lax.scan(
        backward_one,
        jnp.zeros(rel_bias.shape, jnp.float32),
        (queries, key_rows, value_rows, grad_context, segment_now, logsum),
    )
    grad_queries = grads_qkv[0].reshape(seq_count * length, inner_width)
    grad_keys = grads_qkv[1].reshape(seq_count * length, inner_width)
    grad_values = grads_qkv[2].reshape(seq_count * length, inner_width)
    grad_query = matmul_tn(seq_attn, grad_queries)
    grad_key = matmul_tn(seq_attn, grad_keys)
    grad_value = matmul_tn(seq_attn, grad_values)
    grad_normed_attn = (
        matmul_nt(grad_queries, full_query)
        + matmul_nt(grad_keys, full_key)
        + matmul_nt(grad_values, full_value)
    )
    grad_normed_attn = lax.psum_scatter(
        grad_normed_attn.astype(jnp.bfloat16), "tensor", scatter_dimension=0, tiled=True
    ).astype(jnp.float32)
    gain_attn_term = jnp.sum(grad_normed_attn * normed_attn, 0)
    input_grad = grad_middle + rms_back(grad_normed_attn, normed_attn, scale_attn, norm_attn)
    weight_terms = (grad_query, grad_key, grad_value, grad_out, grad_in, grad_back)
    return (output, input_grad, weight_terms, gain_attn_term, gain_ffn_term, bias_sums)


def shards(
    inputs,
    segments,
    norm_attn,
    norm_ffn,
    w_query,
    w_key,
    w_value,
    w_out,
    w_in,
    w_back,
    rel_table,
    cotangent,
):
    micro_count = inputs.shape[0]
    model_width = inputs.shape[2]
    length = segments.shape[2]
    bucket_count = rel_table.shape[0]
    head_local = rel_table.shape[1]
    offsets = jnp.arange(2 * length - 1, dtype=jnp.int32) - (length - 1)
    onehot = (
        bucket_ids(offsets)[:, None] == jnp.arange(bucket_count, dtype=jnp.int32)[None, :]
    ).astype(jnp.float32)
    position = lax.axis_index("tensor") * head_local
    groups_tensor = lax.axis_size("tensor")
    sums_gain_attn = jnp.zeros((model_width,), jnp.float32)
    sums_gain_ffn = sums_gain_attn
    results = []
    grads_in = []

    def gather_rows():
        return (
            lax.all_gather(w_query, "dp", axis=0, tiled=True),
            lax.all_gather(w_key, "dp", axis=0, tiled=True),
            lax.all_gather(w_value, "dp", axis=0, tiled=True),
            lax.all_gather(w_out, "dp", axis=0, tiled=True),
            lax.all_gather(w_in, "dp", axis=0, tiled=True),
            lax.all_gather(w_back, "dp", axis=0, tiled=True),
        )

    rel_bias = bias_planes(rel_table, onehot, length)
    weight_sums = (jnp.zeros((model_width, w_query.shape[1]), jnp.float32),) * 4 + (
        jnp.zeros((model_width, w_in.shape[1]), jnp.float32),
    ) * 2
    bias_total = jnp.zeros(rel_bias.shape, jnp.float32)
    for micro_index in range(micro_count):
        output, input_grad, weight_terms, gain_attn_term, gain_ffn_term, bias_sums = one_micro(
            inputs[micro_index].astype(jnp.float32),
            cotangent[micro_index],
            segments[micro_index],
            gather_rows,
            rel_bias,
            norm_attn,
            norm_ffn,
        )
        results.append(output)
        grads_in.append(input_grad)
        weight_sums = tuple((total + term for total, term in zip(weight_sums, weight_terms)))
        sums_gain_attn = sums_gain_attn + gain_attn_term
        sums_gain_ffn = sums_gain_ffn + gain_ffn_term
        bias_total = bias_total + bias_sums
    summed = lax.psum_scatter(weight_sums, "dp", scatter_dimension=0, tiled=True)
    table_local = bias_table(bias_total, onehot, length)
    table_full = lax.dynamic_update_slice_in_dim(
        jnp.zeros((bucket_count, head_local * groups_tensor), jnp.float32), table_local, position, 1
    )
    output_all = jnp.stack(results)
    input_grad_all = jnp.stack(grads_in)
    gain_attn_grad, gain_ffn_grad, table_sum = lax.psum(
        (sums_gain_attn, sums_gain_ffn, table_full), ("dp", "tensor")
    )
    table_grad = lax.dynamic_slice_in_dim(table_sum, position, head_local, 1)
    return (
        output_all,
        input_grad_all,
        gain_attn_grad,
        gain_ffn_grad,
        summed[0],
        summed[1],
        summed[2],
        summed[3],
        summed[4],
        summed[5],
        table_grad,
    )


def solution(mesh):
    return jax.shard_map(
        shards,
        mesh=mesh,
        in_specs=(
            P(None, ("dp", "tensor"), None),
            P(None, "dp", None),
            P(),
            P(),
            P("dp", "tensor"),
            P("dp", "tensor"),
            P("dp", "tensor"),
            P("dp", "tensor"),
            P("dp", "tensor"),
            P("dp", "tensor"),
            P(None, "tensor"),
            P(None, ("dp", "tensor"), None),
        ),
        out_specs=(
            P(None, ("dp", "tensor"), None),
            P(None, ("dp", "tensor"), None),
            P(),
            P(),
            P("dp", "tensor"),
            P("dp", "tensor"),
            P("dp", "tensor"),
            P("dp", "tensor"),
            P("dp", "tensor"),
            P("dp", "tensor"),
            P(None, "tensor"),
        ),
        check_vma=False,
    )
```

profile of v0, /device:TPU:0, one launch (start us, length us, event | category | flops | bytes accessed | tf_op | source)
XLA Modules:
  0.0 1393.1 jit_solution(3340551342618479803)
XLA Ops:
  14.1 24.8 %all_gather.30 = bf16[768,384]{1,0:T(8,128)(2,1)S(1)} all-gather(bf16[48,384]{1,0:T(8,128)(2,1)S(1)} %copy-done.59), channel_id=1, replica_groups=mesh['dp'=16,'tensor'=2] {'dp'}, dimensions={0}, use_global_device_ids=true | all-gather | bytes 626688 | tf_op jit(solution)/shard_map/all_gather | solution.py:235
  38.9 19.0 %all_gather.31 = bf16[768,384]{1,0:T(8,128)(2,1)S(1)} all-gather(bf16[48,384]{1,0:T(8,128)(2,1)S(1)} %copy-done.60), channel_id=1, replica_groups=mesh['dp'=16,'tensor'=2] {'dp'}, dimensions={0}, use_global_device_ids=true | all-gather | bytes 626688 | tf_op jit(solution)/shard_map/all_gather | solution.py:236
  57.9 20.4 %all_gather.29 = bf16[768,384]{1,0:T(8,128)(2,1)S(1)} all-gather(bf16[48,384]{1,0:T(8,128)(2,1)S(1)} %copy-done.61), channel_id=1, replica_groups=mesh['dp'=16,'tensor'=2] {'dp'}, dimensions={0}, use_global_device_ids=true | all-gather | bytes 626688 | tf_op jit(solution)/shard_map/all_gather | solution.py:237
  78.4 20.4 %all_gather.64 = bf16[768,384]{1,0:T(8,128)(2,1)} all-gather(bf16[48,384]{1,0:T(8,128)(2,1)S(1)} %copy-done.62), channel_id=1, replica_groups=mesh['dp'=16,'tensor'=2] {'dp'}, dimensions={0}, use_global_device_ids=true | all-gather | bytes 626688 | tf_op jit(solution)/shard_map/all_gather | solution.py:238
  101.5 210.0 %while.6 = (s32[]{:T(128)}, f32[6,1024,1024]{1,2,0:T(8,128)}, f32[6,2047]{1,0:T(8,128)S(1)}, s32[]{:T(128)}, f32[1]{0:T(128)}) while((s32[]{:T(128)}, f32[6,1024,1024]{1,2,0:T(8,128)}, f32[6,2047]{1,0:T(8,128)S(1)}, s32[]{:T(128)}, f32[1]{0:T(128)}) %tuple.86), condition=%wide.region_2.3_spmd, body=%wide.region_1.2_spmd.sunk | while | flops 2050 | bytes 83910720 | solution.py:71
  109.1 12.4 reshape.282
  144.2 12.4 reshape.282
  179.1 12.4 reshape.282
  214.2 12.4 reshape.282
  249.1 12.4 reshape.282
  284.2 12.4 reshape.282
  316.5 19.6 %fusion.88 = (f32[6,1024]{1,0:T(8,128)S(1)}, f32[6,1024,1024]{1,2,0:T(8,128)}) fusion(f32[6,1024,1024]{1,2,0:T(8,128)} %get-tuple-element.189, bf16[1024,6,64]{0,2,1:T(8,128)(2,1)} %bitcast.220, bf16[1024,6,64]{0,2,1:T(8,128)(2,1)} %bitcast.218, pred[1024,1024]{0,1:T(8,128)(4,1)} %broadcast_compare_fusion), kind=kOutput, calls=%fused_computation.166 | convolution fusion | flops 824174592 | bytes 52977664 | tf_op jit(solution)/shard_map/while/body/eval_jaxpr/qhe,khe->hqk/dot_general | solution.py:81
  336.1 10.2 exponential_reduce_fusion
  347.2 10.6 fusion.64
  366.4 17.1 %fusion.87 = (f32[6,1024]{1,0:T(8,128)S(1)}, f32[6,1024,1024]{1,2,0:T(8,128)}) fusion(f32[6,1024,1024]{1,2,0:T(8,128)} %get-tuple-element.189, bf16[1024,6,64]{0,2,1:T(8,128)(2,1)S(1)} %bitcast.224, bf16[1024,6,64]{0,2,1:T(8,128)(2,1)S(1)} %bitcast.222, pred[1024,1024]{0,1:T(8,128)(4,1)} %broadcast_compare_fusion.1), kind=kOutput, calls=%fused_computation.165 | convolution fusion | flops 824174592 | bytes 52977664 | tf_op jit(solution)/shard_map/while/body/eval_jaxpr/qhe,khe->hqk/dot_general | solution.py:81
  383.6 10.4 exponential_reduce_fusion.1
  394.9 10.6 fusion.58
  413.9 38.2 %reduce-scatter.17.cloned.1.call-done = f32[512,768]{1,0:T(8,128)} async-done(((f32[1024,768]{1,0:T(8,128)}), f32[512,768]{1,0:T(8,128)}) %reduce-scatter.17.cloned.1.call-update) | async-done | bytes 1572880 | tf_op jit(solution)/shard_map/reduce_scatter | solution.py:142
  458.0 22.7 %all-gather.27.cloned.1.call-done = bf16[1024,768]{1,0:T(8,128)(2,1)} async-done(((bf16[512,768]{1,0:T(8,128)(2,1)}), bf16[1024,768]{1,0:T(8,128)(2,1)}) %all-gather.27.cloned.1.call-update) | async-done | bytes 1572880 | tf_op jit(solution)/shard_map/all_gather | solution.py:130
  480.7 44.4 %all-gather.17.cloned.1.call-done = bf16[768,1536]{1,0:T(8,128)(2,1)} async-done(((bf16[48,1536]{1,0:T(8,128)(2,1)}), bf16[768,1536]{1,0:T(8,128)(2,1)}) %all-gather.17.cloned.1.call-update) | async-done | bytes 2359312 | tf_op jit(solution)/shard_map/all_gather | solution.py:240
  525.1 7.4 fusion.94
  532.5 35.9 %all-gather.15.cloned.1.call-done = bf16[768,1536]{1,0:T(8,128)(2,1)} async-done(((bf16[48,1536]{1,0:T(8,128)(2,1)}), bf16[768,1536]{1,0:T(8,128)(2,1)}) %all-gather.15.cloned.1.call-update) | async-done | bytes 2359312 | tf_op jit(solution)/shard_map/all_gather | solution.py:239
  568.4 28.1 %all-gather.21.cloned.1.call-done = bf16[1024,768]{1,0:T(8,128)(2,1)} async-done(((bf16[512,768]{1,0:T(8,128)(2,1)}), bf16[1024,768]{1,0:T(8,128)(2,1)}) %all-gather.21.cloned.1.call-update) | async-done | bytes 1572880 | tf_op jit(solution)/shard_map/all_gather | solution.py:147
  596.5 11.3 fusion.9
  613.2 12.1 all-gather.23.cloned.1.call-done
  625.3 7.5 fusion.91
  632.8 21.7 %all-gather.13.cloned.1.call-done = bf16[1024,768]{1,0:T(8,128)(2,1)} async-done(((bf16[512,768]{1,0:T(8,128)(2,1)}), bf16[1024,768]{1,0:T(8,128)(2,1)}) %all-gather.13.cloned.1.call-update) | async-done | bytes 1572880 | tf_op jit(solution)/shard_map/all_gather | solution.py:147
  654.5 11.2 fusion.5
  671.2 8.6 convolution_convert_fusion.3
  683.5 28.3 %reduce-scatter.25.cloned.1.call-done = bf16[512,768]{1,0:T(8,128)(2,1)} async-done(((bf16[1024,768]{1,0:T(8,128)(2,1)}), bf16[512,768]{1,0:T(8,128)(2,1)}) %reduce-scatter.25.cloned.1.call-update) | async-done | bytes 786448 | tf_op jit(solution)/shard_map/reduce_scatter | solution.py:162
  714.9 25.2 %reduce-scatter.19.cloned.1.call-done = bf16[512,768]{1,0:T(8,128)(2,1)} async-done(((bf16[1024,768]{1,0:T(8,128)(2,1)}), bf16[512,768]{1,0:T(8,128)(2,1)}) %reduce-scatter.19.cloned.1.call-update) | async-done | bytes 786448 | tf_op jit(solution)/shard_map/reduce_scatter | solution.py:152
  745.2 26.5 %all-gather.29.cloned.1.call-done = bf16[1024,768]{1,0:T(8,128)(2,1)} async-done(((bf16[512,768]{1,0:T(8,128)(2,1)}), bf16[1024,768]{1,0:T(8,128)(2,1)}) %all-gather.29.cloned.1.call-update) | async-done | bytes 1572880 | tf_op jit(solution)/shard_map/all_gather | solution.py:168
  774.1 11.2 fusion.67
  785.3 15.9 %multiply_reduce_fusion = (f32[6,1024]{1,0:T(8,128)S(1)}, f32[6,1024,1024]{1,2,0:T(8,128)}) fusion(f32[6,1024,1024]{1,2,0:T(8,128)} %get-tuple-element.287, f32[6,1024]{1,0:T(8,128)S(1)} %copy-done.50, bf16[1024,6,64]{0,2,1:T(8,128)(2,1)S(1)} %bitcast.213, bf16[1024,6,64]{0,2,1:T(8,128)(2,1)S(1)} %bitcast.207), kind=kOutput, calls=%fused_computation.8 | convolution fusion | flops 824174592 | bytes 51953664 | tf_op jit(solution)/shard_map/while/body/eval_jaxpr/qhe,khe->hqk/dot_general | solution.py:99
  803.6 15.8 %multiply_reduce_fusion.1 = (f32[6,1024]{1,0:T(8,128)S(1)}, f32[6,1024,1024]{1,2,0:T(8,128)}) fusion(f32[6,1024,1024]{1,2,0:T(8,128)} %get-tuple-element.285, f32[6,1024]{1,0:T(8,128)S(1)} %log_add_fusion.1, bf16[1024,6,64]{0,2,1:T(8,128)(2,1)S(1)} %bitcast.210, bf16[1024,6,64]{0,2,1:T(8,128)(2,1)S(1)} %bitcast.209), kind=kOutput, calls=%fused_computation.10 | convolution fusion | flops 824174592 | bytes 51953664 | tf_op jit(solution)/shard_map/while/body/eval_jaxpr/qhe,khe->hqk/dot_general | solution.py:99
  819.4 50.6 %convert_add_fusion = (f32[6,1024,1024]{1,2,0:T(8,128)}, bf16[6,1024,1024]{1,2,0:T(8,128)(2,1)}, bf16[6,1024,1024]{1,2,0:T(8,128)(2,1)}) fusion(f32[6,1024,1024]{1,2,0:T(8,128)} %get-tuple-element.293, f32[6,1024]{1,0:T(8,128)S(1)} %get-tuple-element.292, f32[6,1024,1024]{1,2,0:T(8,128)} %get-tuple-element.285, f32[6,1024]{1,0:T(8,128)S(1)} %log_add_fusion.1, ...), kind=kLoop, calls=%fused_computation.6 | loop fusion | flops 69206016 | bytes 151093248 | tf_op jit(solution)/shard_map/add | solution.py:263
  870.1 8.9 convolution_convert_fusion.12
  887.7 8.6 convolution_convert_fusion.14
  897.8 7.1 convolution_convert_fusion.15
  908.4 13.5 fusion.61
  926.8 8.6 convolution_convert_fusion.2
  970.6 8.7 add_bitcast_fusion
  986.1 292.8 %while.7 = (s32[]{:T(128)}, f32[6,2047]{1,0:T(8,128)S(1)}, f32[6,1024,1024]{1,2,0:T(8,128)}, s32[]{:T(128)}, f32[]{:T(128)}, /*index=5*/s32[]{:T(128)}) while((s32[]{:T(128)}, f32[6,2047]{1,0:T(8,128)S(1)}, f32[6,1024,1024]{1,2,0:T(8,128)}, s32[]{:T(128)}, f32[]{:T(128)}, /*index=5*/s32[]{:T(128)}) %tuple.89), condition=%wide.region_38.39_spmd, body=%wide.region_36.38_spmd.sunk | while | flops 2095106 | bytes 88088664 | solution.py:75
  996.6 6.8 pad.32
  1003.4 11.6 reshape.283
  1021.6 9.3 reshape.284
  1051.8 11.6 reshape.283
  1063.5 6.7 pad.33
  1070.2 9.2 reshape.284
  1100.4 11.6 reshape.283
  1111.9 6.8 pad.33
  1118.7 9.3 reshape.284
  1148.9 11.5 reshape.283
  1160.5 6.7 pad.33
  1167.2 9.3 reshape.284
  1197.6 11.5 reshape.283
  1209.1 6.7 pad.33
  1215.9 9.2 reshape.284
  1239.4 6.9 pad.32
  1246.3 12.0 reshape.283
  1258.3 7.3 pad.33
  1265.5 9.2 reshape.284
  1282.5 40.8 %all-reduce.2 = (f32[768]{0:T(1024)}, f32[768]{0:T(1024)}, f32[32,12]{0,1:T(8,128)S(1)}) all-reduce(f32[768]{0:T(1024)S(1)} %add.314, f32[768]{0:T(1024)S(1)} %add.315, f32[32,12]{0,1:T(8,128)S(1)} %dynamic_update_slice.36), channel_id=1, replica_groups=mesh['dp'=16,'tensor'=2] {'dp','tensor'}, use_global_device_ids=true, to_apply=%region_26.27 | all-reduce | flops 1920 | bytes 15360 | tf_op jit(solution)/shard_map/psum | solution.py:271
  1336.0 50.0 %reduce-scatter.43.cloned.1.call-done = f32[48,1536]{1,0:T(8,128)} async-done(((f32[768,1536]{1,0:T(8,128)}), f32[48,1536]{1,0:T(8,128)}) %reduce-scatter.43.cloned.1.call-update) | async-done | bytes 294928
  (375 shorter events, 397.1 us)
Async XLA Ops:
  7.2 93.2 %copy-start = (f32[32,6]{0,1:T(8,128)S(1)}, f32[32,6]{0,1:T(8,128)}, u32[]{:S(2)}) copy-start(f32[32,6]{0,1:T(8,128)} %param.26) | copy-start | bytes 2308
  7.2 31.7 %copy-start.60 = (bf16[48,384]{1,0:T(8,128)(2,1)S(1)}, bf16[48,384]{1,0:T(8,128)(2,1)}, u32[]{:S(2)}) copy-start(bf16[48,384]{1,0:T(8,128)(2,1)} %param.21) | copy-start | bytes 110596
  7.2 304.3 %all-gather.19.cloned.1.call-start = ((), (), s32[]{:S(2)}) async-start(), calls=%async_computation.20 | async-start | bytes 2359296 | tf_op jit(solution)/shard_map/all_gather | solution.py:129
  9.0 48.9 %copy-start.61 = (bf16[48,384]{1,0:T(8,128)(2,1)S(1)}, bf16[48,384]{1,0:T(8,128)(2,1)}, u32[]{:S(2)}) copy-start(bf16[48,384]{1,0:T(8,128)(2,1)} %param.22) | copy-start | bytes 110596
  9.7 68.7 %copy-start.62 = (bf16[48,384]{1,0:T(8,128)(2,1)S(1)}, bf16[48,384]{1,0:T(8,128)(2,1)}, u32[]{:S(2)}) copy-start(bf16[48,384]{1,0:T(8,128)(2,1)} %param.23) | copy-start | bytes 110596
  12.6 350.6 %all-gather.11.cloned.1.call-start = ((), (), s32[]{:S(2)}) async-start(), calls=%async_computation.14 | async-start | bytes 2359296 | tf_op jit(solution)/shard_map/all_gather | solution.py:129
  13.4 400.5 %reduce-scatter.21.cloned.1.call-start = ((), (), s32[]{:S(2)}) async-start(), calls=%async_computation.21 | async-start | bytes 4718592 | tf_op jit(solution)/shard_map/reduce_scatter | solution.py:142
  13.4 88.1 %copy-start.74 = (s32[2047]{0:T(1024)}, s32[2047]{0:T(1024)S(1)}, u32[]{:S(2)}) copy-start(s32[2047]{0:T(1024)S(1)} %fusion.73) | copy-start | bytes 24568
  38.9 326.7 %copy-start.23 = (bf16[768,384]{1,0:T(8,128)(2,1)}, bf16[768,384]{1,0:T(8,128)(2,1)S(1)}, u32[]{:S(2)}) copy-start(bf16[768,384]{1,0:T(8,128)(2,1)S(1)} %all_gather.30) | copy-start | bytes 1769476
  57.9 305.2 %copy-start.26 = (bf16[768,384]{1,0:T(8,128)(2,1)}, bf16[768,384]{1,0:T(8,128)(2,1)S(1)}, u32[]{:S(2)}) copy-start(bf16[768,384]{1,0:T(8,128)(2,1)S(1)} %all_gather.31) | copy-start | bytes 1769476
  78.4 315.6 %copy-start.21 = (bf16[768,384]{1,0:T(8,128)(2,1)}, bf16[768,384]{1,0:T(8,128)(2,1)S(1)}, u32[]{:S(2)}) copy-start(bf16[768,384]{1,0:T(8,128)(2,1)S(1)} %all_gather.29) | copy-start | bytes 1769476
  347.2 10.7 copy-start.34
  347.2 10.7 copy-start.49
  347.2 11.6 copy-start.29
  361.5 90.5 %reduce-scatter.17.cloned.1.call-start = ((), (), s32[]{:S(2)}) async-start(), calls=%async_computation.15 | async-start | bytes 4718592 | tf_op jit(solution)/shard_map/reduce_scatter | solution.py:142
  365.6 18.0 %copy-start.44 = (bf16[1024,384]{0,1:T(8,128)(2,1)}, bf16[1024,384]{0,1:T(8,128)(2,1)S(1)}, u32[]{:S(2)}) copy-start(bf16[1024,384]{0,1:T(8,128)(2,1)S(1)} %convolution_convert_fusion.9) | copy-start | bytes 2359300
  366.4 17.1 %copy-start.46 = (bf16[1024,384]{0,1:T(8,128)(2,1)}, bf16[1024,384]{0,1:T(8,128)(2,1)S(1)}, u32[]{:S(2)}) copy-start(bf16[1024,384]{0,1:T(8,128)(2,1)S(1)} %convolution_convert_fusion.10) | copy-start | bytes 2359300
  383.6 10.4 copy-start.79
  394.9 10.6 copy-start.36
  409.1 43.0 %copy-start.3 = (bf16[2,512,768]{2,1,0:T(8,128)(2,1)S(1)}, bf16[2,512,768]{2,1,0:T(8,128)(2,1)}, u32[]{:S(2)}) copy-start(bf16[2,512,768]{2,1,0:T(8,128)(2,1)} %param.16) | copy-start | bytes 4718596
  409.1 71.6 %all-gather.27.cloned.1.call-start = ((), (), s32[]{:S(2)}) async-start(), calls=%async_computation.28 | async-start | bytes 2359296 | tf_op jit(solution)/shard_map/all_gather | solution.py:130
  412.4 112.6 %all-gather.17.cloned.1.call-start = ((), (), s32[]{:S(2)}) async-start(), calls=%async_computation.18 | async-start | bytes 2506752 | tf_op jit(solution)/shard_map/all_gather | solution.py:240
  413.0 155.4 %all-gather.15.cloned.1.call-start = ((), (), s32[]{:S(2)}) async-start(), calls=%async_computation.17 | async-start | bytes 2506752 | tf_op jit(solution)/shard_map/all_gather | solution.py:239
  413.8 41.9 %copy-start.51 = (f32[768]{0:T(1024)S(1)}, f32[768]{0:T(1024)}, u32[]{:S(2)}) copy-start(f32[768]{0:T(1024)} %param.19) | copy-start | bytes 9220
  413.8 182.7 %all-gather.21.cloned.1.call-start = ((), (), s32[]{:S(2)}) async-start(), calls=%async_computation.22 | async-start | bytes 2359296 | tf_op jit(solution)/shard_map/all_gather | solution.py:147
  454.4 285.7 %copy-start.5 = (f32[512,768]{1,0:T(8,128)}, f32[512,768]{1,0:T(8,128)S(1)}, u32[]{:S(2)}) copy-start(f32[512,768]{1,0:T(8,128)S(1)} %get-tuple-element.277) | copy-start | bytes 4718596
  454.5 285.7 %copy-start.54 = (f32[512]{0:T(512)}, f32[512]{0:T(512)S(1)}, u32[]{:S(2)}) copy-start(f32[512]{0:T(512)S(1)} %get-tuple-element.296) | copy-start | bytes 6148
  454.5 285.6 %copy-start.56 = (f32[512]{0:T(512)}, f32[512]{0:T(512)S(1)}, u32[]{:S(2)}) copy-start(f32[512]{0:T(512)S(1)} %get-tuple-element.297) | copy-start | bytes 6148
  457.2 168.1 %all-gather.23.cloned.1.call-start = ((), (), s32[]{:S(2)}) async-start(), calls=%async_computation.24 | async-start | bytes 2359296 | tf_op jit(solution)/shard_map/all_gather | solution.py:130
  457.9 196.6 %all-gather.13.cloned.1.call-start = ((), (), s32[]{:S(2)}) async-start(), calls=%async_computation.16 | async-start | bytes 2359296 | tf_op jit(solution)/shard_map/all_gather | solution.py:147
  532.4 151.0 %reduce-scatter.29.cloned.1.call-start = ((), (), s32[]{:S(2)}) async-start(), calls=%async_computation.29 | async-start | bytes 2359296 | tf_op jit(solution)/shard_map/reduce_scatter | solution.py:162
  596.5 12.9 copy-start.76
  613.1 98.6 %reduce-scatter.25.cloned.1.call-start = ((), (), s32[]{:S(2)}) async-start(), calls=%async_computation.25 | async-start | bytes 2359296 | tf_op jit(solution)/shard_map/reduce_scatter | solution.py:162
  654.5 12.9 copy-start.77
  671.1 69.0 %reduce-scatter.19.cloned.1.call-start = ((), (), s32[]{:S(2)}) async-start(), calls=%async_computation.19 | async-start | bytes 2359296 | tf_op jit(solution)/shard_map/reduce_scatter | solution.py:152
  671.2 40.6 %copy-start.8 = (f32[512,768]{1,0:T(8,128)S(1)}, f32[512,768]{1,0:T(8,128)}, u32[]{:S(2)}) copy-start(f32[512,768]{1,0:T(8,128)} %copy-done.7) | copy-start | bytes 4718596
  679.8 91.9 %all-gather.29.cloned.1.call-start = ((), (), s32[]{:S(2)}) async-start(), calls=%async_computation.30 | async-start | bytes 2359296 | tf_op jit(solution)/shard_map/all_gather | solution.py:168
  714.9 29.4 %copy-start.67 = (f32[512]{0:T(512)}, f32[512]{0:T(512)S(1)}, u32[]{:S(2)}) copy-start(f32[512]{0:T(512)S(1)} %broadcast_multiply_fusion.1) | copy-start | bytes 6148
  714.9 29.4 %copy-start.69 = (f32[512]{0:T(512)}, f32[512]{0:T(512)S(1)}, u32[]{:S(2)}) copy-start(f32[512]{0:T(512)S(1)} %broadcast_multiply_fusion.3) | copy-start | bytes 6148
  744.3 29.8 %copy-start.50 = (f32[6,1024]{1,0:T(8,128)S(1)}, f32[6,1024]{1,0:T(8,128)}, u32[]{:S(2)}) copy-start(f32[6,1024]{1,0:T(8,128)} %copy-done.49) | copy-start | bytes 73732
  744.3 56.9 %all-gather.25.cloned.1.call-start = ((), (), s32[]{:S(2)}) async-start(), calls=%async_computation.26 | async-start | bytes 2359296 | tf_op jit(solution)/shard_map/all_gather | solution.py:168
  744.9 534.8 %reduce-scatter.31.cloned.1.call-start = ((), (), s32[]{:S(2)}) async-start(), calls=%async_computation.31 | async-start | bytes 2359296 | tf_op jit(solution)/shard_map/reduce_scatter | solution.py:194
  774.1 11.2 copy-start.35
  785.3 99.9 %copy-start.11 = (bf16[6,64,1024]{2,1,0:T(8,128)(2,1)}, bf16[6,64,1024]{2,1,0:T(8,128)(2,1)S(1)}, u32[]{:S(2)}) copy-start(bf16[6,64,1024]{2,1,0:T(8,128)(2,1)S(1)} %fusion.67) | copy-start | bytes 2359300
  785.3 15.9 %copy-start.30 = (bf16[768,384]{1,0:T(8,128)(2,1)S(1)}, bf16[768,384]{1,0:T(8,128)(2,1)}, u32[]{:S(2)}) copy-start(bf16[768,384]{1,0:T(8,128)(2,1)} %all_gather.64) | copy-start | bytes 1769476
  803.6 15.9 %copy-start.38 = (bf16[1024,384]{0,1:T(8,128)(2,1)}, bf16[1024,384]{0,1:T(8,128)(2,1)S(1)}, u32[]{:S(2)}) copy-start(bf16[1024,384]{0,1:T(8,128)(2,1)S(1)} %convolution_convert_fusion.5) | copy-start | bytes 2359300
  870.1 8.9 copy-start.2
  887.5 392.3 %reduce-scatter.27.cloned.1.call-start = ((), (), s32[]{:S(2)}) async-start(), calls=%async_computation.27 | async-start | bytes 2359296 | tf_op jit(solution)/shard_map/reduce_scatter | solution.py:194
  926.5 402.1 %reduce-scatter.23.cloned.1.call-start = ((), (), s32[]{:S(2)}) async-start(), calls=%async_computation.23 | async-start | bytes 2359296 | tf_op jit(solution)/shard_map/reduce_scatter | solution.py:152
  935.4 400.6 %reduce-scatter.39.cloned.1.call-start = ((), (), s32[]{:S(2)}) async-start(), calls=%async_computation.35 | async-start | bytes 1253376 | tf_op jit(solution)/shard_map/reduce_scatter | solution.py:264
  939.3 396.7 %reduce-scatter.37.cloned.1.call-start = ((), (), s32[]{:S(2)}) async-start(), calls=%async_computation.34 | async-start | bytes 1253376 | tf_op jit(solution)/shard_map/reduce_scatter | solution.py:264
  944.1 391.9 %reduce-scatter.35.cloned.1.call-start = ((), (), s32[]{:S(2)}) async-start(), calls=%async_computation.33 | async-start | bytes 1253376 | tf_op jit(solution)/shard_map/reduce_scatter | solution.py:264
  948.8 387.2 %reduce-scatter.33.cloned.1.call-start = ((), (), s32[]{:S(2)}) async-start(), calls=%async_computation.32 | async-start | bytes 1253376 | tf_op jit(solution)/shard_map/reduce_scatter | solution.py:264
  953.4 382.6 %reduce-scatter.41.cloned.1.call-start = ((), (), s32[]{:S(2)}) async-start(), calls=%async_computation.36 | async-start | bytes 5013504 | tf_op jit(solution)/shard_map/reduce_scatter | solution.py:264
  963.6 422.5 %reduce-scatter.43.cloned.1.call-start = ((), (), s32[]{:S(2)}) async-start(), calls=%async_computation.37 | async-start | bytes 5013504
  986.1 292.9 %copy-start.75 = (s32[2047]{0:T(1024)S(1)}, s32[2047]{0:T(1024)}, u32[]{:S(2)}) copy-start(s32[2047]{0:T(1024)} %copy-done.74) | copy-start | bytes 24568
  986.1 293.7 %copy-start.4 = (bf16[2,512,768]{2,1,0:T(8,128)(2,1)S(1)}, bf16[2,512,768]{2,1,0:T(8,128)(2,1)}, u32[]{:S(2)}) copy-start(bf16[2,512,768]{2,1,0:T(8,128)(2,1)} %param.16) | copy-start | bytes 4718596
  986.1 293.7 %copy-start.53 = (f32[768]{0:T(1024)S(1)}, f32[768]{0:T(1024)}, u32[]{:S(2)}) copy-start(f32[768]{0:T(1024)} %param.18) | copy-start | bytes 9220
  986.1 293.7 %copy-start.64 = (f32[512]{0:T(512)S(1)}, f32[512]{0:T(512)}, u32[]{:S(2)}) copy-start(f32[512]{0:T(512)} %copy-done.63) | copy-start | bytes 6148
  986.1 293.7 %copy-start.66 = (f32[512]{0:T(512)S(1)}, f32[512]{0:T(512)}, u32[]{:S(2)}) copy-start(f32[512]{0:T(512)} %copy-done.65) | copy-start | bytes 6148
  1279.0 44.9 %copy-start.52 = (f32[768]{0:T(1024)S(1)}, f32[768]{0:T(1024)}, u32[]{:S(2)}) copy-start(f32[768]{0:T(1024)} %param.19) | copy-start | bytes 9220
  1279.0 44.9 %copy-start.57 = (f32[512]{0:T(512)S(1)}, f32[512]{0:T(512)}, u32[]{:S(2)}) copy-start(f32[512]{0:T(512)} %copy-done.56) | copy-start | bytes 6148
  1279.0 44.9 %copy-start.70 = (f32[512]{0:T(512)S(1)}, f32[512]{0:T(512)}, u32[]{:S(2)}) copy-start(f32[512]{0:T(512)} %copy-done.69) | copy-start | bytes 6148
  1334.0 52.1 %copy-start.1 = (f32[32,6]{0,1:T(8,128)S(1)}, f32[32,6]{0,1:T(8,128)}, u32[]{:S(2)}) copy-start(f32[32,6]{0,1:T(8,128)} %param.26) | copy-start | bytes 2308
  (46 other events, 154.5 us)
Sparse Core Ops, SparseCore 0:
  12.7 29.8 all-gather.18
  44.2 27.2 all-gather.10
  361.6 41.8 reduce-scatter.20
  409.2 42.7 reduce-scatter.16
  453.4 27.2 all-gather.26
  482.8 42.2 all-gather.16
  527.3 40.9 all-gather.14
  570.5 25.9 all-gather.20
  598.1 27.1 all-gather.22
  627.3 27.2 all-gather.12
  657.3 26.0 reduce-scatter.28
  685.6 26.0 reduce-scatter.24
  714.0 26.0 reduce-scatter.18
  744.5 27.2 all-gather.28
  773.2 27.2 all-gather.24
  887.6 25.9 reduce-scatter.30
  926.7 25.9 reduce-scatter.26
  955.5 26.0 reduce-scatter.22
  985.8 58.0 reduce-scatter.38
  1047.9 56.9 reduce-scatter.36
  1109.2 57.0 reduce-scatter.34
  1170.5 57.0 reduce-scatter.32
  1232.0 74.7 reduce-scatter.40
  1311.6 74.4 reduce-scatter.42
where the time goes:
time: 1400 us; the launch traced here: 1390 us
  local copies, waits for them, and re-layouts  501 us (36%)
  waiting for transfers between devices  340 us (24%)
  matrix products  280 us (20%)
  other arithmetic  129 us (9%)
  blocking collectives  126 us (9%)
  between operations  15.8 us (1%)
    reshape x6, local copies, waits for them, and re-layouts, toeplitz_rows(): return window.reshape(length, 2 * length - 1)[:, :length]  74.5 us
    reshape x6, local copies, waits for them, and re-layouts, diagonal_sums(): widened = jnp.pad(matrix, ((0, 0), (0, length - 1))).reshape(-1)  69.8 us
    dynamic_slice x12, local copies, waits for them, and re-layouts, bias_table(): diagonals = lax.map(lambda matrix: diagonal_sums(matrix, length), bias_sums)  61.4 us
    dynamic_update_slice x12, local copies, waits for them, and re-layouts, bias_planes(): return lax.map(lambda column: toeplitz_rows(column, length), per_offset.T)  60.7 us
    reshape x6, local copies, waits for them, and re-layouts, diagonal_sums(): placed = jnp.pad(widened, (length - 1, 1)).reshape(length, 2 * length)  55.5 us
    unnamed x25, waiting for transfers between devices  53.5 us
    dot_general x12, matrix products, matmul(): return jnp.dot(left, right, preferred_element_type=jnp.float32)  51.9 us
    add x1, other arithmetic, shards(): bias_total = bias_total + bias_sums  50.6 us
  transfers between devices with their start and end apart: 24, of which 12 were waited for; matrix products, arithmetic and copies ran while one was open for 58% of the time, Pallas kernels for 0%

commit v1 on v0

v1 whole, which is shorter than its diff:
```python
import functools

import jax
import jax.numpy as jnp
from jax import lax
from jax.experimental import pallas as pl
from jax.experimental.pallas import tpu as pltpu
from jax.sharding import PartitionSpec as P

MESH = pl.DeviceIdType.MESH
BF = jnp.bfloat16
F32 = jnp.float32
HIGHEST = lax.Precision.HIGHEST
EPSILON = 1e-06
THRESHOLDS = (12, 16, 23, 32, 46, 64, 91)
MASK_OUT = -float(2**30)
DH = 64
SPAN = 512
LANES = 128
VMEM_BYTES = 62 * 2**20


def nn(left, right):
    return lax.dot_general(left, right, (((1,), (0,)), ((), ())), preferred_element_type=F32)


def nt(left, right):
    return lax.dot_general(left, right, (((1,), (1,)), ((), ())), preferred_element_type=F32)


def tn(left, right):
    return lax.dot_general(left, right, (((0,), (0,)), ((), ())), preferred_element_type=F32)


def iota(shape, dim):
    return lax.broadcasted_iota(jnp.int32, shape, dim)


def bucket_ids(offsets):
    distance = jnp.abs(offsets)
    far_ids = 8 + sum((distance >= threshold).astype(jnp.int32) for threshold in THRESHOLDS)
    return jnp.where(offsets > 0, 16, 0) + jnp.where(distance < 8, distance, far_ids)


def rms_scale(values):
    return lax.rsqrt(jnp.mean(values * values, -1, keepdims=True) + EPSILON)


def rms_back(grad_normed, normed, scale, gain):
    scaled = grad_normed * gain
    return scale * (scaled - normed * jnp.mean(scaled * normed, -1, keepdims=True))


def gelu_pair(v):
    square = v * v
    half = 0.5 + 0.5 * jnp.tanh(v * (0.7978845608028654 + 0.035677408136300125 * square))
    slope = half + v * half * (1.0 - half) * (1.5957691216057308 + 0.2140644488178007 * square)
    return v * half, slope


class Place:
    def __init__(self, depth):
        d, t = lax.axis_index("dp"), lax.axis_index("tensor")
        self.t = t
        self.z, self.y, self.c = lax.div(d, 4), lax.rem(lax.div(d, 2), 2), lax.rem(d, 2)
        self.depth = depth
        self.sib = (d + 1 - 2 * self.c, t)
        self.ypeer = (d + 2 - 4 * self.y, t)
        self.xpeer = (d, 1 - t)
        rest = lax.rem(d, 4)
        self.zs = [lax.rem(self.z + step, depth) for step in range(1, depth)]
        self.zpeers = [(z * 4 + rest, t) for z in self.zs]

    def barrier(self):
        semaphore = pltpu.get_barrier_semaphore()
        peers = [self.sib, self.ypeer, self.xpeer] + self.zpeers
        for peer in peers:
            pl.semaphore_signal(semaphore, inc=1, device_id=peer, device_id_type=MESH)
        pl.semaphore_wait(semaphore, len(peers))


class Copy:
    def __init__(self, **parts):
        self.parts = parts

    def made(self):
        return pltpu.make_async_remote_copy(device_id_type=MESH, **self.parts)

    def start(self):
        self.made().start()

    def wait_recv(self):
        self.made().wait_recv()

    def wait_send(self):
        self.made().wait_send()


def remote(src, dst, sems, index, peer):
    send, recv = sems
    return Copy(
        src_ref=src, dst_ref=dst, send_sem=send.at[index], recv_sem=recv.at[index], device_id=peer
    )


class Gather:
    def __init__(self, place, ref, width, sems, item, x_first):
        self.p, self.ref, self.width, self.sems, self.item = place, ref, width, sems, item
        self.x_first = x_first
        self.first, self.second = (
            (place.xpeer, place.ypeer) if x_first else (place.ypeer, place.xpeer)
        )

    def cols(self, x):
        return pl.ds(pl.multiple_of(x * self.width, LANES), self.width)

    def region(self, y, x):
        return self.ref.at[:, y, self.p.c, :, self.cols(x)]

    def send(self, index, src, peer):
        return remote(src, src, self.sems, (self.item, index), peer)

    def copies(self):
        p = self.p
        own = self.ref.at[p.z, p.y, p.c, :, self.cols(p.t)]
        regions = [self.region(p.y, p.t)]
        regions.append(self.region(p.y, 1 - p.t) if self.x_first else self.region(1 - p.y, p.t))
        regions.append(self.region(1 - p.y, p.t) if self.x_first else self.region(p.y, 1 - p.t))
        regions.append(self.region(1 - p.y, 1 - p.t))
        n = len(p.zpeers)
        zs = [self.send(i, own, peer) for i, peer in enumerate(p.zpeers)]
        first = self.send(n, regions[0], self.first)
        seconds = [self.send(n + 1 + i, regions[i], self.second) for i in range(2)]
        sibs = [self.send(n + 3 + i, regions[i], p.sib) for i in range(4)]
        return zs, first, seconds, sibs

    def start(self):
        for copy in self.copies()[0]:
            copy.start()

    def step1(self):
        zs, first, seconds, sibs = self.copies()
        for copy in zs:
            copy.wait_recv()
        first.start()
        seconds[0].start()
        sibs[0].start()

    def step2(self):
        _, first, seconds, sibs = self.copies()
        first.wait_recv()
        seconds[1].start()
        sibs[1].start()

    def step3(self):
        _, _, seconds, sibs = self.copies()
        seconds[0].wait_recv()
        sibs[2].start()
        seconds[1].wait_recv()
        sibs[3].start()

    def finish(self):
        zs, first, seconds, sibs = self.copies()
        for copy in sibs:
            copy.wait_recv()
        for copy in zs + [first] + seconds + sibs:
            copy.wait_send()


def gather_sems(items, depth):
    return [pltpu.SemaphoreType.DMA((items, depth + 6))] * 2


class Scatter:
    def __init__(self, place, ref, width, bufs, sems, item, y_first):
        self.p, self.ref, self.width, self.sems, self.item = place, ref, width, sems, item
        self.r0, self.r1, self.r2, self.r3 = bufs
        self.y_first = y_first

    def cols(self, x):
        return pl.ds(pl.multiple_of(x * self.width, LANES), self.width)

    def copies(self):
        p, ref = self.p, self.ref
        sib = remote(ref.at[:, :, 1 - p.c], self.r0, self.sems, (self.item, 0), p.sib)
        if self.y_first:
            half = remote(ref.at[:, 1 - p.y, p.c], self.r1, self.sems, (self.item, 1), p.ypeer)
            quarter = remote(
                ref.at[:, p.y, p.c, :, self.cols(1 - p.t)],
                self.r2,
                self.sems,
                (self.item, 2),
                p.xpeer,
            )
        else:
            half = remote(
                ref.at[:, :, p.c, :, self.cols(1 - p.t)],
                self.r1,
                self.sems,
                (self.item, 1),
                p.xpeer,
            )
            quarter = remote(
                ref.at[:, 1 - p.y, p.c, :, self.cols(p.t)],
                self.r2,
                self.sems,
                (self.item, 2),
                p.ypeer,
            )
        zs = [
            remote(
                ref.at[z, p.y, p.c, :, self.cols(p.t)],
                self.r3.at[i],
                self.sems,
                (self.item, 3 + i),
                peer,
            )
            for i, (z, peer) in enumerate(zip(p.zs, p.zpeers))
        ]
        return sib, half, quarter, zs

    def step0(self):
        self.copies()[0].start()

    def step1(self):
        p = self.p
        sib, half, _, _ = self.copies()
        sib.wait_recv()
        kept = self.ref.at[:, :, p.c]
        kept[...] = (kept[...].astype(F32) + self.r0[...].astype(F32)).astype(BF)
        half.start()

    def step2(self):
        p = self.p
        _, half, quarter, _ = self.copies()
        half.wait_recv()
        if self.y_first:
            kept = self.ref.at[:, p.y, p.c]
        else:
            kept = self.ref.at[:, :, p.c, :, self.cols(p.t)]
        kept[...] = (kept[...].astype(F32) + self.r1[...].astype(F32)).astype(BF)
        quarter.start()

    def step3(self):
        p = self.p
        _, _, quarter, zs = self.copies()
        quarter.wait_recv()
        kept = self.ref.at[:, p.y, p.c, :, self.cols(p.t)]
        kept[...] = (kept[...].astype(F32) + self.r2[...].astype(F32)).astype(BF)
        for copy in zs:
            copy.start()

    def finish(self, out, offset):
        p = self.p
        sib, half, quarter, zs = self.copies()
        for copy in zs:
            copy.wait_recv()
        total = self.ref[p.z, p.y, p.c, :, self.cols(p.t)].astype(F32)
        for i in range(len(zs)):
            total = total + self.r3[i].astype(F32)
        out[:, pl.ds(pl.multiple_of(offset, LANES), self.width)] = total
        for copy in [sib, half, quarter] + zs:
            copy.wait_send()


def scatter_bufs(items, depth, rows, width, y_first):
    lead = () if items is None else (items,)
    return [
        pltpu.VMEM(lead + (depth, 2, rows, 2 * width), BF),
        pltpu.VMEM(lead + ((depth, rows, 2 * width) if y_first else (depth, 2, rows, width)), BF),
        pltpu.VMEM(lead + (depth, rows, width), BF),
        pltpu.VMEM(lead + (depth - 1, rows, width), BF),
    ]


def scatter_sems(items, depth):
    return [pltpu.SemaphoreType.DMA((items, depth + 2))] * 2


def flat(values):
    if len(values.shape) == 2:
        return values
    return values.reshape(-1, values.shape[-1])


def project_rows(x_rows, gain):
    rows = x_rows.astype(F32)
    return (rows * rms_scale(rows) * gain).astype(BF)


def project(low_ref, w_ref, out_ref):
    weight = flat(w_ref[...])
    half = low_ref.shape[0] // 2

    def one(i, carry):
        rows = pl.ds(pl.multiple_of(i * half, half), half)
        out_ref[rows, :] = nn(low_ref[rows, :], weight).astype(BF)
        return carry

    lax.fori_loop(0, 2, one, 0)


def k1_plain(x_ref, gain_ref, wq_ref, wk_ref, wv_ref, q_ref, k_ref, v_ref, low_ref):
    low_ref[...] = project_rows(x_ref[...], gain_ref[...])
    for weight, out in ((wq_ref, q_ref), (wk_ref, k_ref), (wv_ref, v_ref)):
        project(low_ref, weight, out)


def k1_fused(
    depth,
    x_ref,
    cot_ref,
    gain_ref,
    tab_ref,
    wq_shard,
    wk_shard,
    wv_shard,
    xs_ref,
    cots_ref,
    tabs_ref,
    q_ref,
    k_ref,
    v_ref,
    wq_ref,
    wk_ref,
    wv_ref,
    low_ref,
    g_send,
    g_recv,
    x_send,
    x_recv,
):
    p = Place(depth)
    half_rows = x_ref.shape[1]
    width = wq_shard.shape[1]
    weights = (wq_ref, wk_ref, wv_ref)
    items = [
        Gather(p, ref, width, (g_send, g_recv), i, i != 1) for i, ref in enumerate(weights)
    ]
    for item, shard in zip(items, (wq_shard, wk_shard, wv_shard)):
        item.ref[p.z, p.y, p.c, :, item.cols(p.t)] = shard[...]
    xs_ref[p.t] = x_ref[p.t]
    cots_ref[p.t] = cot_ref[p.t].astype(BF)
    cots_ref[1 - p.t] = cot_ref[1 - p.t].astype(BF)
    tabs_ref[p.t] = tab_ref[...]
    p.barrier()
    for item in items:
        item.start()
    sems = (x_send, x_recv)
    moves = [
        remote(x_ref.at[1 - p.t], xs_ref.at[p.t], sems, 0, p.xpeer),
        remote(tabs_ref.at[p.t], tabs_ref.at[p.t], sems, 1, p.xpeer),
    ]
    moves[0] = remote(x_ref.at[1 - p.t], xs_ref.at[p.t], sems, 0, p.xpeer)
    for move in moves:
        move.start()

    def rows_of(half):
        return pl.ds(pl.multiple_of(half * half_rows, half_rows), half_rows)

    for item in items:
        item.step1()
    low_ref[rows_of(p.t), :] = project_rows(x_ref[p.t], gain_ref[...])
    for item in items:
        item.step2()
    for item in items:
        item.step3()
    moves[0].wait_recv()
    low_ref[rows_of(1 - p.t), :] = project_rows(xs_ref[1 - p.t], gain_ref[...])
    for item, weight, out in zip(items, weights, (q_ref, k_ref, v_ref)):
        item.finish()
        project(low_ref, weight, out)
    moves[1].wait_recv()
    for move in moves:
        move.wait_send()


def bias_rows(tabs_ref, out_ref, flipped):
    offsets = iota((LANES, 4 * LANES), 1) - 2 * LANES
    onehot = (bucket_ids(-offsets if flipped else offsets) == iota((LANES, 4 * LANES), 0)).astype(F32)
    for half in range(2):
        out_ref[half * 8 : half * 8 + 8, :] = jnp.dot(
            tabs_ref[half], onehot, precision=HIGHEST, preferred_element_type=F32
        )


def head_row(pair, per_half):
    return 8 * lax.div(pair, per_half) + 2 * lax.rem(pair, per_half)


def bias_strip(row):
    spread = jnp.broadcast_to(row, (LANES, 4 * LANES))
    return pltpu.roll(spread, 3 * LANES, 1, stride=1, stride_axis=0)


def window(tile, rows, length):
    reach = -(-SPAN // rows)
    return max(0, (tile - reach) * rows), min(length, (tile + reach + 1) * rows)


def segment_lanes(seg_ref, pieces):
    onehot = seg_ref[...] == iota((seg_ref.shape[0], LANES), 1)
    inside = iota((seg_ref.shape[0], LANES), 1) < 16
    return onehot, inside


def pair_cols(pair):
    return pl.ds(pl.multiple_of(pair * LANES, LANES), LANES)


def spread3(value):
    top = value.astype(BF).astype(F32)
    mid = (value - top).astype(BF).astype(F32)
    return top, mid, value - top - mid


def fwd_kernel(
    q_ref, k_ref, v_ref, seg_ref, tabs_ref, ctx_ref, ctxf_ref, feat_ref, bias_ref, segq_ref, segk_ref
):
    length, width = q_ref.shape
    pairs = width // LANES
    per_half = pairs // 2
    tile = 256
    near = SPAN // LANES
    bias_rows(tabs_ref, bias_ref, False)
    onehot, inside = segment_lanes(seg_ref, 1)
    segq_ref[...] = jnp.where(onehot, MASK_OUT, 0.0).astype(BF)
    segk_ref[...] = jnp.where(onehot, 0.0, jnp.where(inside, 1.0, 0.0)).astype(BF)

    def one_pair(pair, carry):
        cols = pair_cols(pair)
        row = head_row(pair, per_half)
        lane = iota((tile, LANES), 1)
        low_half = lane < DH
        strips, fars = [], []
        for hh in range(2):
            line = bias_ref[pl.ds(row + hh, 1), :]
            strips.append(bias_strip(line))
            fars.append((line[:, 0:1], line[:, 4 * LANES - 1 : 4 * LANES]))
        for index in range(length // tile):
            rows = slice(index * tile, (index + 1) * tile)
            start, stop = window(index, tile, length)
            queries = q_ref[rows, cols]
            zero = jnp.zeros_like(queries)
            q_feat = segq_ref[rows, :]
            left = jnp.concatenate(
                [
                    jnp.concatenate([jnp.where(low_half, queries, zero), q_feat], 1),
                    jnp.concatenate([jnp.where(low_half, zero, queries), q_feat], 1),
                ],
                0,
            )
            right = jnp.concatenate([k_ref[start:stop, cols], segk_ref[start:stop, :]], 1)
            scores = nt(left, right)
            weights, peaks = [], []
            for hh in range(2):
                for part in range(tile // LANES):
                    at = hh * tile + part * LANES
                    q_block = index * (tile // LANES) + part
                    blocks = []
                    for k_block in range(start // LANES, stop // LANES):
                        delta = k_block - q_block
                        if abs(delta) > near:
                            blocks.append(None)
                            continue
                        col = k_block * LANES - start
                        block = scores[at : at + LANES, col : col + LANES]
                        if abs(delta) <= 1:
                            block = block + strips[hh][:, (delta + 1) * LANES : (delta + 2) * LANES]
                        else:
                            block = block + fars[hh][0 if delta < 0 else 1]
                        blocks.append(block)
                    real = [block for block in blocks if block is not None]
                    peak = functools.reduce(jnp.maximum, real)
                    peak = jnp.max(peak, -1, keepdims=True)
                    peaks.append(peak)
                    weights.append(
                        jnp.concatenate(
                            [
                                jnp.zeros((LANES, LANES), BF)
                                if block is None
                                else jnp.exp(block - peak).astype(BF)
                                for block in blocks
                            ],
                            1,
                        )
                    )
            values = v_ref[start:stop, cols]
            gathered = nn(
                jnp.concatenate(weights, 0), jnp.concatenate([values, jnp.ones_like(values)], 1)
            )
            normal = gathered[:, :LANES] / gathered[:, LANES:]
            context = jnp.where(low_half, normal[:tile], normal[tile:])
            ctx_ref[rows, cols] = context.astype(BF)
            ctxf_ref[rows, cols] = context
            logs = jnp.concatenate(peaks, 0) + jnp.log(gathered[:, LANES:])
            feature = q_feat.astype(F32)
            for hh in range(2):
                for i, piece in enumerate(spread3(logs[hh * tile : (hh + 1) * tile])):
                    feature = jnp.where(lane == 16 + 3 * hh + i, -piece, feature)
            feat_ref[pair, rows, :] = feature.astype(BF)
        return carry

    lax.fori_loop(0, pairs, one_pair, 0)


def bwd_kernel(
    q_ref,
    k_ref,
    v_ref,
    go_ref,
    ctxf_ref,
    feat_ref,
    seg_ref,
    tabs_ref,
    dq_ref,
    dk_ref,
    dv_ref,
    tabg_ref,
    bias_ref,
    sums_ref,
    far_ref,
    segk_ref,
    gofeat_ref,
    near_ref,
    acc_ref,
):
    length, width = q_ref.shape
    pairs = width // LANES
    per_half = pairs // 2
    tile = 256
    near = SPAN // LANES
    bias_rows(tabs_ref, bias_ref, True)
    sums_ref[...] = jnp.zeros_like(sums_ref)
    far_ref[...] = jnp.zeros_like(far_ref)
    onehot, inside = segment_lanes(seg_ref, 1)
    segk_ref[...] = jnp.where(onehot, 0.0, jnp.where(inside, 1.0, 0.0)).astype(BF)
    flip = (iota((LANES, LANES), 0) + iota((LANES, LANES), 1) == LANES - 1).astype(F32)
    block_of = (lax.div(iota((length, LANES), 0), LANES) == iota((length, LANES), 1)).astype(BF)

    def one_pair(pair, carry):
        cols = pair_cols(pair)
        row = head_row(pair, per_half)
        lane = iota((tile, LANES), 1)
        low_half = lane < DH
        strips, fars = [], []
        for hh in range(2):
            line = bias_ref[pl.ds(row + hh, 1), :]
            strips.append(bias_strip(line))
            fars.append((line[:, 0:1], line[:, 4 * LANES - 1 : 4 * LANES]))
        grads_all = go_ref[:, cols]
        product = grads_all.astype(F32) * ctxf_ref[:, cols]
        lane_all = iota((length, LANES), 1)
        feature = jnp.zeros((length, LANES), F32)
        for hh in range(2):
            keep = (lane_all < DH) if hh == 0 else (lane_all >= DH)
            total = jnp.sum(jnp.where(keep, product, 0.0), -1, keepdims=True)
            for i, piece in enumerate(spread3(total)):
                feature = jnp.where(lane_all == 3 * hh + i, -piece, feature)
        gofeat_ref[...] = feature.astype(BF)
        near_ref[...] = jnp.zeros_like(near_ref)
        acc_ref[...] = jnp.zeros_like(acc_ref)
        far_sums = [[jnp.zeros((1, LANES), F32) for _ in range(2)] for _ in range(2)]
        lane_row = iota((1, LANES), 1)
        for index in range(length // tile):
            rows = slice(index * tile, (index + 1) * tile)
            start, stop = window(index, tile, length)
            keys, values = k_ref[rows, cols], v_ref[rows, cols]
            zero = jnp.zeros_like(keys)
            seg_feat = segk_ref[rows, :].astype(F32)

            def ones_at(base, first):
                return jnp.where((lane >= first) & (lane < first + 3), 1.0, base).astype(BF)

            masked_keys = jnp.concatenate(
                [jnp.where(low_half, keys, zero), jnp.where(low_half, zero, keys)], 0
            )
            masked_values = jnp.concatenate(
                [jnp.where(low_half, values, zero), jnp.where(low_half, zero, values)], 0
            )
            key_feats = jnp.concatenate([ones_at(seg_feat, 16), ones_at(seg_feat, 19)], 0)
            value_feats = jnp.concatenate([ones_at(0.0, 0), ones_at(0.0, 3)], 0)
            queries = q_ref[start:stop, cols]
            grads = go_ref[start:stop, cols]
            logits = nt(
                jnp.concatenate([masked_keys, key_feats], 1),
                jnp.concatenate([queries, feat_ref[pair, start:stop, :]], 1),
            )
            shifted = nt(
                jnp.concatenate([masked_values, value_feats], 1),
                jnp.concatenate([grads, gofeat_ref[start:stop, :]], 1),
            )
            probs_rows, score_rows = [], []
            for hh in range(2):
                for part in range(tile // LANES):
                    at = hh * tile + part * LANES
                    k_block = index * (tile // LANES) + part
                    probs, score_grads = [], []
                    for q_block in range(start // LANES, stop // LANES):
                        delta = k_block - q_block
                        if abs(delta) > near:
                            probs.append(jnp.zeros((LANES, LANES), BF))
                            score_grads.append(jnp.zeros((LANES, LANES), BF))
                            continue
                        col = q_block * LANES - start
                        block = logits[at : at + LANES, col : col + LANES]
                        place = (1 - delta) * LANES
                        if abs(delta) <= 1:
                            block = block + strips[hh][:, place : place + LANES]
                        else:
                            block = block + fars[hh][0 if delta > 0 else 1]
                        prob = jnp.exp(block)
                        grad = prob * shifted[at : at + LANES, col : col + LANES]
                        if abs(delta) <= 1:
                            near_ref[hh, :, place : place + LANES] += grad
                        probs.append(prob.astype(BF))
                        score_grads.append(grad.astype(BF))
                    probs_rows.append(jnp.concatenate(probs, 1))
                    score_rows.append(jnp.concatenate(score_grads, 1))
            probs_all = jnp.concatenate(probs_rows, 0)
            scores_all = jnp.concatenate(score_rows, 0)
            value_grad = nn(probs_all, grads)
            dv_ref[rows, cols] = jnp.where(low_half, value_grad[:tile], value_grad[tile:]).astype(BF)
            key_grad = nn(scores_all, jnp.concatenate([queries, block_of[start:stop]], 1))
            dk_ref[rows, cols] = jnp.where(
                low_half, key_grad[:tile, :LANES], key_grad[tile:, :LANES]
            ).astype(BF)
            acc_ref[start:stop, :] += tn(scores_all, masked_keys)
            for hh in range(2):
                for part in range(tile // LANES):
                    at = hh * tile + part * LANES
                    k_block = index * (tile // LANES) + part
                    line = jnp.sum(key_grad[at : at + LANES, LANES:], 0, keepdims=True)
                    far_sums[hh][0] += jnp.where(lane_row <= k_block - 2, line, 0.0)
                    far_sums[hh][1] += jnp.where(lane_row >= k_block + 2, line, 0.0)
        dq_ref[:, cols] = acc_ref[...].astype(BF)
        for hh in range(2):
            turned = jnp.dot(flip, near_ref[hh], precision=HIGHEST, preferred_element_type=F32)
            turned = jnp.concatenate([turned, jnp.zeros((LANES, LANES), F32)], 1)
            turned = pltpu.roll(turned, 1, 1, stride=1, stride_axis=0)
            sums_ref[pl.ds(row + hh, 1), :] = jnp.sum(turned, 0, keepdims=True)
            last = lane_row == 0
            positive = jnp.sum(far_sums[hh][0], -1, keepdims=True)
            negative = jnp.sum(far_sums[hh][1], -1, keepdims=True)
            far_ref[pl.ds(row + hh, 1), :] = jnp.where(last, positive, jnp.where(lane_row == 1, negative, 0.0))
        return carry

    lax.fori_loop(0, pairs, one_pair, 0)
    offsets = 2 * LANES - iota((LANES, 4 * LANES), 1)
    onehot_buckets = (bucket_ids(offsets) == iota((LANES, 4 * LANES), 0)).astype(F32)
    table = lax.dot_general(
        sums_ref[...],
        onehot_buckets,
        (((1,), (1,)), ((), ())),
        precision=HIGHEST,
        preferred_element_type=F32,
    )
    lane = iota(tabg_ref.shape, 1)
    far = far_ref[...]
    table = table + jnp.where(lane == 31, far[:, 0:1], 0.0) + jnp.where(lane == 15, far[:, 1:2], 0.0)
    tabg_ref[...] = table


def k3_before(xs_ref, ctx_ref, wo, gain, middle_ref, ffn_ref, ffnt_ref):
    step = 256

    def one(i, carry):
        rows = pl.ds(pl.multiple_of(i * step, step), step)
        middle = xs_ref[rows, :].astype(F32) + nt(ctx_ref[rows, :], wo)
        middle_ref[rows, :] = middle
        low = (middle * rms_scale(middle) * gain).astype(BF)
        ffn_ref[rows, :] = low
        ffnt_ref[:, rows] = low.T
        return carry

    lax.fori_loop(0, middle_ref.shape[0] // step, one, 0)


def transpose_rows(src_ref, dst_ref):
    step = 256

    def one(i, carry):
        rows = pl.ds(pl.multiple_of(i * step, step), step)
        dst_ref[:, rows] = src_ref[rows, :].T
        return carry

    lax.fori_loop(0, src_ref.shape[0] // step, one, 0)


def ffn_rows(i, half, w_in, w_back, first, ffn_ref, cot_ref, hid_ref, gp_ref, up_ref, down_ref):
    rows = pl.ds(pl.multiple_of(i * half, half), half)
    hidden, slope = gelu_pair(nn(ffn_ref[rows, :], w_in))
    hidden = hidden.astype(BF)
    hid_ref[rows, :] = hidden
    grad_pre = (nn(cot_ref[rows, :], w_back) * slope).astype(BF)
    gp_ref[rows, :] = grad_pre
    up = nt(hidden, w_back)
    down = nt(grad_pre, w_in)
    keep = jnp.where(first, 0.0, 1.0).astype(F32)

    @pl.when(first)
    def _():
        up_ref[rows, :] = up
        down_ref[rows, :] = down

    @pl.when(jnp.logical_not(first))
    def _():
        up_ref[rows, :] += up
        down_ref[rows, :] += down


def after_rows(rows, cot, up_ref, down_ref, gain, gain_ref, gm_ref, ca_ref, cat_ref):
    middle = gm_ref[rows, :]
    scale = rms_scale(middle)
    normed = middle * scale
    down = down_ref[rows, :]
    gain_ref[...] += jnp.sum(down * normed, 0, keepdims=True)
    grad = cot + rms_back(down, normed, scale, gain)
    gm_ref[rows, :] = grad
    low = grad.astype(BF)
    ca_ref[rows, :] = low
    cat_ref[:, rows] = low.T
    return middle + up_ref[rows, :]


def context_grad(ca_ref, wo, go_ref):
    step = 256

    def one(i, carry):
        rows = pl.ds(pl.multiple_of(i * step, step), step)
        go_ref[rows, :] = nn(ca_ref[rows, :], wo).astype(BF)
        return carry

    lax.fori_loop(0, ca_ref.shape[0] // step, one, 0)


def k3_fused(
    depth,
    xs_ref,
    ctx_ref,
    cot_ref,
    cots_ref,
    gain_ref,
    wo_shard,
    wi_shard,
    wb_shard,
    out_ref,
    gm_ref,
    go_ref,
    ggain_ref,
    gwo_ref,
    gwi_ref,
    gwb_ref,
    wo_ref,
    wi_ref,
    wb_ref,
    ffn_ref,
    ffnt_ref,
    cott_ref,
    cotb_ref,
    hid_ref,
    gp_ref,
    up_ref,
    down_ref,
    obuf_ref,
    obuf2_ref,
    o0,
    o1,
    o2,
    o3,
    i0,
    i1,
    i2,
    i3,
    b0,
    b1,
    b2,
    b3,
    g_send,
    g_recv,
    s_send,
    s_recv,
    x_send,
    x_recv,
):
    p = Place(depth)
    length = ctx_ref.shape[0]
    half_rows = length // 2
    width = wo_shard.shape[1]
    chunks = wi_ref.shape[0]
    part = wi_shard.shape[1] // chunks
    g_sems, s_sems, x_sems = (g_send, g_recv), (s_send, s_recv), (x_send, x_recv)

    def part_cols(k):
        return pl.ds(pl.multiple_of(k * part, LANES), part)

    g_out = Gather(p, wo_ref, width, g_sems, 0, True)

    def g_chunk(k):
        return (
            Gather(p, wi_ref.at[k], part, g_sems, 1 + 2 * k, True),
            Gather(p, wb_ref.at[k], part, g_sems, 2 + 2 * k, False),
        )

    def s_chunk(k):
        return (
            Scatter(
                p, wi_ref.at[k], part, [r.at[k] for r in (i0, i1, i2, i3)], s_sems, 1 + 2 * k, True
            ),
            Scatter(
                p, wb_ref.at[k], part, [r.at[k] for r in (b0, b1, b2, b3)], s_sems, 2 + 2 * k, False
            ),
        )

    def when_gather(k, name):
        @pl.when(k < chunks)
        def _():
            for item in g_chunk(k):
                getattr(item, name)()

    def when_scatter(k, name):
        @pl.when((k >= 0) & (k < chunks))
        def _():
            for item, out in zip(s_chunk(k), (gwi_ref, gwb_ref)):
                if name == "finish":
                    item.finish(out, k * part)
                else:
                    getattr(item, name)()

    wo_ref[p.z, p.y, p.c, :, g_out.cols(p.t)] = wo_shard[...]
    for k in range(chunks):
        for item, shard in zip(g_chunk(k), (wi_shard, wb_shard)):
            item.ref[p.z, p.y, p.c, :, item.cols(p.t)] = shard[:, k * part : (k + 1) * part]
    p.barrier()
    g_out.start()
    for k in range(2):
        when_gather(k, "start")
    cot_move = remote(cots_ref.at[1 - p.t], cotb_ref.at[p.t], x_sems, 0, p.xpeer)
    cot_move.start()
    cotb_ref[p.t] = cots_ref[p.t]
    for k in range(2, chunks):
        when_gather(k, "start")
    g_out.step1()
    when_gather(0, "step1")
    when_gather(1, "step1")
    g_out.step2()
    when_gather(0, "step2")
    g_out.step3()
    when_gather(2, "step1")
    when_gather(1, "step2")
    when_gather(0, "step3")
    g_out.finish()
    gain = gain_ref[...]
    k3_before(xs_ref, ctx_ref, flat(wo_ref[...]), gain, gm_ref, ffn_ref, ffnt_ref)
    cot_move.wait_recv()
    cotb = cotb_ref.reshape(length, cotb_ref.shape[2])
    transpose_rows(cotb, cott_ref)

    def one_chunk(k, carry):
        when_gather(k + 3, "step1")
        when_gather(k + 2, "step2")
        when_gather(k + 1, "step3")
        for item in g_chunk(k):
            item.finish()
        when_scatter(k - 2, "step2")
        w_in, w_back = flat(wi_ref[k]), flat(wb_ref[k])
        args = (w_in, w_back, k == 0, ffn_ref, cotb, hid_ref, gp_ref, up_ref, down_ref)
        ffn_rows(0, half_rows, *args)
        when_scatter(k - 1, "step1")
        ffn_rows(1, half_rows, *args)
        when_scatter(k - 3, "step3")
        wb_ref[k] = nn(cott_ref[...], hid_ref[...]).astype(BF).reshape(wb_ref.shape[1:])
        when_scatter(k - 4, "finish")
        wi_ref[k] = nn(ffnt_ref[...], gp_ref[...]).astype(BF).reshape(wi_ref.shape[1:])
        for item in s_chunk(k):
            item.step0()
        return carry

    lax.fori_loop(0, chunks, one_chunk, 0)
    when_scatter(chunks - 1, "step1")
    when_scatter(chunks - 2, "step2")
    when_scatter(chunks - 3, "step3")
    ggain_ref[...] = jnp.zeros_like(ggain_ref)
    step = 256

    def finish_rows(own, i):
        half = p.t if own else 1 - p.t
        at = pl.ds(pl.multiple_of(i * step, step), step)
        rows = pl.ds(pl.multiple_of(half * half_rows + i * step, step), step)
        cot = cot_ref[p.t, at, :] if own else cotb_ref[1 - p.t, at, :].astype(F32)
        out = after_rows(
            rows, cot, up_ref, down_ref, gain, ggain_ref, gm_ref, ffn_ref, cott_ref
        )
        if own:
            out_ref[p.t, at, :] = out
        else:
            obuf_ref[at, :] = out.astype(BF)

    for i in range(half_rows // step):
        finish_rows(False, i)
    out_move = remote(obuf_ref, obuf2_ref, x_sems, 1, p.xpeer)
    out_move.start()
    for i in range(half_rows // step):
        finish_rows(True, i)
    when_scatter(chunks - 4, "finish")
    when_scatter(chunks - 1, "step2")
    context_grad(ffn_ref, flat(wo_ref[...]), go_ref)
    when_scatter(chunks - 2, "step3")
    wo_ref[...] = nn(cott_ref[...], ctx_ref[...]).astype(BF).reshape(wo_ref.shape)
    s_out = Scatter(p, wo_ref, width, (o0, o1, o2, o3), s_sems, 0, True)
    s_out.step0()
    when_scatter(chunks - 3, "finish")
    s_out.step1()
    when_scatter(chunks - 1, "step3")
    when_scatter(chunks - 2, "finish")
    s_out.step2()
    s_out.step3()
    out_move.wait_recv()
    out_ref[1 - p.t] = obuf2_ref[...].astype(F32)
    when_scatter(chunks - 1, "finish")
    s_out.finish(gwo_ref, 0)
    cot_move.wait_send()
    out_move.wait_send()


def k3_plain(
    xs_ref,
    ctx_ref,
    cot_ref,
    gain_ref,
    wo_ref,
    wi_ref,
    wb_ref,
    out_ref,
    gm_ref,
    go_ref,
    ggain_ref,
    gwo_ref,
    gwi_ref,
    gwb_ref,
    ffn_ref,
    ffnt_ref,
    cott_ref,
    cotb_ref,
    hid_ref,
    gp_ref,
    up_ref,
    down_ref,
):
    length = ctx_ref.shape[0]
    half_rows = length // 2
    chunk = hid_ref.shape[1]
    gain = gain_ref[...]
    cotb_ref[...] = cot_ref[...].astype(BF)
    k3_before(xs_ref, ctx_ref, wo_ref[...], gain, gm_ref, ffn_ref, ffnt_ref)
    transpose_rows(cotb_ref, cott_ref)

    def one_chunk(k, carry):
        cols = pl.ds(pl.multiple_of(k * chunk, LANES), chunk)
        w_in, w_back = wi_ref[:, cols], wb_ref[:, cols]
        for i in range(2):
            ffn_rows(
                i, half_rows, w_in, w_back, k == 0, ffn_ref, cotb_ref, hid_ref, gp_ref, up_ref, down_ref
            )
        gwb_ref[:, cols] = nn(cott_ref[...], hid_ref[...]).astype(BF)
        gwi_ref[:, cols] = nn(ffnt_ref[...], gp_ref[...]).astype(BF)
        return carry

    lax.fori_loop(0, wi_ref.shape[1] // chunk, one_chunk, 0)
    ggain_ref[...] = jnp.zeros_like(ggain_ref)
    step = 256

    def finish_rows(i, carry):
        rows = pl.ds(pl.multiple_of(i * step, step), step)
        out_ref[rows, :] = after_rows(
            rows,
            cot_ref[rows, :],
            up_ref,
            down_ref,
            gain,
            ggain_ref,
            gm_ref,
            ffn_ref,
            cott_ref,
        )
        return carry

    lax.fori_loop(0, length // step, finish_rows, 0)
    context_grad(ffn_ref, wo_ref[...], go_ref)
    gwo_ref[...] = nn(cott_ref[...], ctx_ref[...]).astype(BF)


def low_transposed(xs_ref, gain, lowt_ref):
    step = 256

    def one(i, carry):
        rows = pl.ds(pl.multiple_of(i * step, step), step)
        lowt_ref[:, rows] = project_rows(xs_ref[rows, :], gain).T
        return carry

    lax.fori_loop(0, xs_ref.shape[0] // step, one, 0)


def input_rows(rows, xs_ref, gm_ref, grads, weights, gain, gain_out):
    down = sum(nt(grad[rows, :], flat(weight[...])) for grad, weight in zip(grads, weights))
    inputs = xs_ref[rows, :].astype(F32)
    scale = rms_scale(inputs)
    normed = inputs * scale
    gain_out[...] += jnp.sum(down * normed, 0, keepdims=True)
    return gm_ref[rows, :] + rms_back(down, normed, scale, gain)


def k5_fused(
    depth,
    xs_ref,
    gm_ref,
    dq_ref,
    dk_ref,
    dv_ref,
    wq_ref,
    wk_ref,
    wv_ref,
    gain_ref,
    ggain_ref,
    tabg_ref,
    ig_ref,
    gwq_ref,
    gwk_ref,
    gwv_ref,
    small_ref,
    lowt_ref,
    gq_ref,
    gk_ref,
    gv_ref,
    ibuf_ref,
    ibuf2_ref,
    again_ref,
    sm_ref,
    smr_ref,
    a0,
    a1,
    a2,
    a3,
    c0,
    c1,
    c2,
    c3,
    d0,
    d1,
    d2,
    d3,
    s_send,
    s_recv,
    x_send,
    x_recv,
):
    p = Place(depth)
    length = xs_ref.shape[0]
    half_rows = length // 2
    width = gwq_ref.shape[1]
    s_sems, x_sems = (s_send, s_recv), (x_send, x_recv)
    items = [
        Scatter(p, gq_ref, width, (a0, a1, a2, a3), s_sems, 0, True),
        Scatter(p, gk_ref, width, (c0, c1, c2, c3), s_sems, 1, False),
        Scatter(p, gv_ref, width, (d0, d1, d2, d3), s_sems, 2, True),
    ]
    gain = gain_ref[...]
    p.barrier()
    low_transposed(xs_ref, gain, lowt_ref)
    for item, grad in zip(items, (dq_ref, dk_ref, dv_ref)):
        item.ref[...] = nn(lowt_ref[...], grad[...]).astype(BF).reshape(item.ref.shape)
        item.step0()
        if item is not items[0]:
            items[items.index(item) - 1].step1()
    again_ref[...] = jnp.zeros_like(again_ref)
    step = 256
    grads, weights = (dq_ref, dk_ref, dv_ref), (wq_ref, wk_ref, wv_ref)

    def finish_rows(own, i):
        half = p.t if own else 1 - p.t
        at = pl.ds(pl.multiple_of(i * step, step), step)
        rows = pl.ds(pl.multiple_of(half * half_rows + i * step, step), step)
        out = input_rows(rows, xs_ref, gm_ref, grads, weights, gain, again_ref)
        if own:
            ig_ref[p.t, at, :] = out
        else:
            ibuf_ref[at, :] = out.astype(BF)

    for i in range(half_rows // step):
        finish_rows(False, i)
    move = remote(ibuf_ref, ibuf2_ref, x_sems, 0, p.xpeer)
    move.start()
    items[2].step1()
    items[0].step2()
    for i in range(half_rows // step):
        finish_rows(True, i)
    model = again_ref.shape[1]
    sm_ref[0, 0:1, :model] = again_ref[...]
    sm_ref[0, 1:2, :model] = ggain_ref[...]
    sm_ref[0, 2:8, :model] = jnp.zeros((6, model), F32)
    sm_ref[0, :, model : model + LANES] = tabg_ref[0:8, :]
    sm_ref[0, :, model + LANES :] = tabg_ref[8:16, :]
    hops = [(p.sib,), (p.ypeer,), (p.xpeer,), tuple(p.zpeers)]
    slot = 0
    comm = [
        lambda: items[1].step2(),
        lambda: items[0].step3(),
        lambda: items[2].step2(),
        lambda: items[1].step3(),
    ]
    for level, peers in enumerate(hops):
        moves = [
            remote(sm_ref.at[level], smr_ref.at[slot + i], x_sems, 1 + slot + i, peer)
            for i, peer in enumerate(peers)
        ]
        for one in moves:
            one.start()
        comm[level]()
        total = sm_ref[level]
        for i, one in enumerate(moves):
            one.wait_recv()
            total = total + smr_ref[slot + i]
        slot += len(peers)
        if level + 1 < len(hops):
            sm_ref[level + 1] = total
        else:
            small_ref[...] = total
        for one in moves:
            one.wait_send()
    items[2].step3()
    move.wait_recv()
    ig_ref[1 - p.t] = ibuf2_ref[...].astype(F32)
    for item, out in zip(items, (gwq_ref, gwk_ref, gwv_ref)):
        item.finish(out, 0)
    move.wait_send()


def k5_plain(
    xs_ref,
    gm_ref,
    dq_ref,
    dk_ref,
    dv_ref,
    wq_ref,
    wk_ref,
    wv_ref,
    gain_ref,
    ig_ref,
    gwq_ref,
    gwk_ref,
    gwv_ref,
    again_ref,
    lowt_ref,
):
    gain = gain_ref[...]
    low_transposed(xs_ref, gain, lowt_ref)
    grads, weights = (dq_ref, dk_ref, dv_ref), (wq_ref, wk_ref, wv_ref)
    for grad, out in zip(grads, (gwq_ref, gwk_ref, gwv_ref)):
        out[...] = nn(lowt_ref[...], grad[...]).astype(BF)
    again_ref[...] = jnp.zeros_like(again_ref)
    step = 256

    def one(i, carry):
        rows = pl.ds(pl.multiple_of(i * step, step), step)
        ig_ref[rows, :] = input_rows(rows, xs_ref, gm_ref, grads, weights, gain, again_ref)
        return carry

    lax.fori_loop(0, xs_ref.shape[0] // step, one, 0)


def call(kernel, outs, scratch, args, name, collective=None):
    spec = pl.BlockSpec(memory_space=pltpu.VMEM)
    if collective is None:
        params = pltpu.CompilerParams(vmem_limit_bytes=VMEM_BYTES)
    else:
        params = pltpu.CompilerParams(
            vmem_limit_bytes=VMEM_BYTES, collective_id=collective, has_side_effects=True
        )
    return pl.pallas_call(
        kernel,
        out_shape=[jax.ShapeDtypeStruct(shape, dtype) for shape, dtype in outs],
        in_specs=[spec] * len(args),
        out_specs=[spec] * len(outs),
        scratch_shapes=scratch,
        compiler_params=params,
        name=name,
    )(*args)


def shards(
    inputs,
    segments,
    norm_attn,
    norm_ffn,
    w_query,
    w_key,
    w_value,
    w_out,
    w_in,
    w_back,
    rel_table,
    cotangent,
):
    dp, tensor = lax.axis_size("dp"), lax.axis_size("tensor")
    t = lax.axis_index("tensor")
    rows, width = w_query.shape
    hidden_part = w_in.shape[1]
    model = inputs.shape[2]
    length = segments.shape[2]
    half = inputs.shape[1]
    buckets, heads = rel_table.shape
    depth = dp // 4
    fused = rows % 16 == 0 and dp % 4 == 0 and depth >= 2
    gain_attn, gain_ffn = norm_attn.reshape(1, model), norm_ffn.reshape(1, model)
    table = jnp.pad(rel_table.T, ((0, 8 - heads), (0, LANES - buckets)))
    segment = lax.dynamic_index_in_dim(segments[:, 0], t, 0, False).reshape(length, 1)
    full = (length, model)
    inner = (length, width * tensor)
    square = (depth, 2, 2, rows, 2 * width)
    part = 256
    chunks = hidden_part // part
    dma = pltpu.SemaphoreType.DMA
    if fused:
        xs, cots, tabs, queries, keys, values, wq, wk, wv = call(
            functools.partial(k1_fused, depth),
            [
                ((2, half, model), BF),
                ((2, half, model), BF),
                ((2, 8, LANES), F32),
                (inner, BF),
                (inner, BF),
                (inner, BF),
                (square, BF),
                (square, BF),
                (square, BF),
            ],
            [pltpu.VMEM(full, BF)] + gather_sems(3, depth) + [dma((2,)), dma((2,))],
            (inputs, cotangent, gain_attn, table, w_query, w_key, w_value),
            "exchange_project",
            0,
        )
        xs = xs.reshape(full)
    else:

        def whole(weight):
            weight = lax.all_gather(weight, "dp", axis=0, tiled=True)
            return lax.all_gather(weight, "tensor", axis=1, tiled=True)

        def exchanged(local):
            own = lax.dynamic_index_in_dim(local, t, 0, False)
            other = lax.dynamic_index_in_dim(local, 1 - t, 0, False)
            other = lax.ppermute(other, "tensor", [(0, 1), (1, 0)])
            first = jnp.where(t == 0, own, other)
            second = jnp.where(t == 0, other, own)
            return jnp.concatenate([first, second], 0)

        def returned(seq):
            mine = lax.dynamic_slice_in_dim(seq, t * half, half, 0)
            other = lax.dynamic_slice_in_dim(seq, (1 - t) * half, half, 0)
            other = lax.ppermute(other, "tensor", [(0, 1), (1, 0)])
            return jnp.stack([jnp.where(t == 0, mine, other), jnp.where(t == 0, other, mine)])

        def scattered(grad):
            grad = lax.psum_scatter(grad.astype(F32), "tensor", scatter_dimension=1, tiled=True)
            return lax.psum_scatter(grad, "dp", scatter_dimension=0, tiled=True)

        xs = exchanged(inputs)
        tabs = lax.all_gather(table, "tensor", axis=0)
        wq, wk, wv, wo, wi, wb = (
            whole(w) for w in (w_query, w_key, w_value, w_out, w_in, w_back)
        )
        queries, keys, values = call(
            k1_plain,
            [(inner, BF)] * 3,
            [pltpu.VMEM(full, BF)],
            (xs, gain_attn, wq, wk, wv),
            "project",
        )
    pairs = inner[1] // LANES
    ctx, ctxf, feats = call(
        fwd_kernel,
        [(inner, BF), (inner, F32), ((pairs, length, LANES), BF)],
        [pltpu.VMEM((16, 4 * LANES), F32)] + [pltpu.VMEM((length, LANES), BF)] * 2,
        (queries, keys, values, segment, tabs),
        "attention_forward",
    )
    work = [
        pltpu.VMEM(full, BF),
        pltpu.VMEM((model, length), BF),
        pltpu.VMEM((model, length), BF),
    ]
    rest = [
        pltpu.VMEM((length, 2 * part), BF),
        pltpu.VMEM((length, 2 * part), BF),
        pltpu.VMEM(full, F32),
        pltpu.VMEM(full, F32),
    ]
    if fused:
        big = pltpu.VMEM((chunks, depth, 2, 2, rows, 2 * part), BF)
        output, grad_middle, grad_context, ggain, gwo, gwi, gwb = call(
            functools.partial(k3_fused, depth),
            [
                ((2, half, model), F32),
                (full, F32),
                (inner, BF),
                ((1, model), F32),
                ((rows, width), F32),
                ((rows, hidden_part), F32),
                ((rows, hidden_part), F32),
            ],
            [pltpu.VMEM(square, BF), big, big]
            + work
            + [pltpu.VMEM((2, half, model), BF)]
            + rest
            + [pltpu.VMEM((half, model), BF)] * 2
            + scatter_bufs(None, depth, rows, width, True)
            + scatter_bufs(chunks, depth, rows, part, True)
            + scatter_bufs(chunks, depth, rows, part, False)
            + gather_sems(1 + 2 * chunks, depth)
            + scatter_sems(1 + 2 * chunks, depth)
            + [dma((2,)), dma((2,))],
            (xs, ctx, cotangent, cots, gain_ffn, w_out, w_in, w_back),
            "feed_forward",
            1,
        )
    else:
        out_seq, grad_middle, grad_context, ggain, gwo, gwi, gwb = call(
            k3_plain,
            [
                (full, F32),
                (full, F32),
                (inner, BF),
                ((1, model), F32),
                (wo.shape, BF),
                (wi.shape, BF),
                (wb.shape, BF),
            ],
            work + [pltpu.VMEM(full, BF)] + rest,
            (xs, ctx, exchanged(cotangent), gain_ffn, wo, wi, wb),
            "feed_forward",
        )
        output = returned(out_seq)
        gwo, gwi, gwb = scattered(gwo), scattered(gwi), scattered(gwb)
    dq, dk, dv, table_grad = call(
        bwd_kernel,
        [(inner, BF), (inner, BF), (inner, BF), ((16, LANES), F32)],
        [
            pltpu.VMEM((16, 4 * LANES), F32),
            pltpu.VMEM((16, 4 * LANES), F32),
            pltpu.VMEM((16, LANES), F32),
            pltpu.VMEM((length, LANES), BF),
            pltpu.VMEM((length, LANES), BF),
            pltpu.VMEM((2, LANES, 3 * LANES), F32),
            pltpu.VMEM((length, LANES), F32),
        ],
        (queries, keys, values, grad_context, ctxf, feats, segment, tabs),
        "attention_backward",
    )
    if fused:
        input_grad, gwq, gwk, gwv, small = call(
            functools.partial(k5_fused, depth),
            [
                ((2, half, model), F32),
                ((rows, width), F32),
                ((rows, width), F32),
                ((rows, width), F32),
                ((8, model + 2 * LANES), F32),
            ],
            [pltpu.VMEM((model, length), BF)]
            + [pltpu.VMEM(square, BF)] * 3
            + [pltpu.VMEM((half, model), BF)] * 2
            + [
                pltpu.VMEM((1, model), F32),
                pltpu.VMEM((4, 8, model + 2 * LANES), F32),
                pltpu.VMEM((depth + 2, 8, model + 2 * LANES), F32),
            ]
            + scatter_bufs(None, depth, rows, width, True)
            + scatter_bufs(None, depth, rows, width, False)
            + scatter_bufs(None, depth, rows, width, True)
            + scatter_sems(3, depth)
            + [dma((depth + 3,)), dma((depth + 3,))],
            (xs, grad_middle, dq, dk, dv, wq, wk, wv, gain_attn, ggain, table_grad),
            "projection_gradients",
            2,
        )
        gain_attn_grad, gain_ffn_grad = small[0, :model], small[1, :model]
        tables = jnp.stack([small[:, model : model + LANES], small[:, model + LANES :]])
    else:
        ig_seq, gwq, gwk, gwv, again = call(
            k5_plain,
            [(full, F32), (wq.shape, BF), (wk.shape, BF), (wv.shape, BF), ((1, model), F32)],
            [pltpu.VMEM((model, length), BF)],
            (xs, grad_middle, dq, dk, dv, wq, wk, wv, gain_attn),
            "projection_gradients",
        )
        input_grad = returned(ig_seq)
        gwq, gwk, gwv = scattered(gwq), scattered(gwk), scattered(gwv)
        again, ggain, tables = lax.psum((again, ggain, table_grad), ("dp", "tensor"))
        gain_attn_grad, gain_ffn_grad = again[0], ggain[0]
        tables = tables.reshape(2, 8, LANES)
    table_out = lax.dynamic_index_in_dim(tables, t, 0, False)[:heads, :buckets].T
    return (
        output,
        input_grad,
        gain_attn_grad,
        gain_ffn_grad,
        gwq,
        gwk,
        gwv,
        gwo,
        gwi,
        gwb,
        table_out,
    )


def solution(mesh):
    weight = P("dp", "tensor")
    tokens = P(None, ("dp", "tensor"), None)
    return jax.shard_map(
        shards,
        mesh=mesh,
        in_specs=(
            tokens,
            P(None, "dp", None),
            P(),
            P(),
            weight,
            weight,
            weight,
            weight,
            weight,
            weight,
            P(None, "tensor"),
            tokens,
        ),
        out_specs=(
            tokens,
            tokens,
            P(),
            P(),
            weight,
            weight,
            weight,
            weight,
            weight,
            weight,
            P(None, "tensor"),
        ),
        check_vma=False,
    )
```

time: 1400 us -> 340 us (0.24)
  local copies, waits for them, and re-layouts: 501 us -> 17.1 us
  waiting for transfers between devices: 340 us -> 0 us
  Pallas kernels: 0 us -> 322 us
  matrix products: 280 us -> 0 us
  other arithmetic: 129 us -> 0.01 us
  blocking collectives: 126 us -> 0 us
  between operations: 15.8 us -> 0.72 us
    pallas_call x0 -> x5, Pallas kernels: none -> 322 us  [call(): pl.pallas_call(kernel, out_shape=[jax.ShapeDtypeStruct(shape, dtype) for...]
    dot_general x50 -> x0, matrix products: 280 us -> none  [the longest x12 51.9 us: matmul(): return jnp.dot(left, right, preferred_element_type=jnp.float32)]
    reshape x18 -> x4, local copies, waits for them, and re-layouts: 200 us -> 3.58 us  [the longest x1 1.27 us: shards(): norm_attn.reshape(1, model)]
    all_gather x10 -> x0, waiting for transfers between devices: 191 us -> none  [the longest x2 49.9 us: one_micro(): seq_ffn = lax.all_gather(ffn_low, 'tensor', axis=0, tiled=True)]
    reduce_scatter x13 -> x0, waiting for transfers between devices: 95.4 us -> none  [the longest x2 38.2 us: one_micro(): lax.psum_scatter(attended, 'tensor', scatter_dimension=0, tiled=True)]
    all_gather x4 -> x0, blocking collectives: 84.7 us -> none  [the longest x1 24.8 us: gather_rows(): lax.all_gather(w_query, 'dp', axis=0, tiled=True)]
    pad x12 -> x1, local copies, waits for them, and re-layouts: 81.3 us -> 1.28 us  [shards(): table = jnp.pad(rel_table.T, ((0, 8 - heads), (0, LANES - buckets)))]
    dynamic_slice x19 -> x0, local copies, waits for them, and re-layouts: 62.1 us -> none  [the longest x12 61.4 us: bias_table(): diagonals = lax.map(lambda matrix: diagonal_sums(matrix, length), bias_sums)]
  transfers between devices with their start and end apart: 24 -> 0, of which waited for: 12 -> 0; matrix products, arithmetic and copies ran while one was open for 58% -> 0% of each run, Pallas kernels for 0% -> 0%
where the time goes in v1:
time: 340 us; the launch traced here: 339 us
  Pallas kernels  322 us (95%)
  local copies, waits for them, and re-layouts  17.1 us (5%)
    pallas_call x5, Pallas kernels, call(): pl.pallas_call(kernel, out_shape=[jax.ShapeDtypeStruct(shape, dtype) for...  322 us
    unnamed x24, local copies, waits for them, and re-layouts  9.57 us

profile of v1, /device:TPU:0, one launch (start us, length us, event | category | flops | bytes accessed | tf_op | source)
XLA Modules:
  0.0 339.4 jit_solution(14638004268184512748)
XLA Ops:
  0.6 0.0 copy-start
  0.7 1.3 reshape.37.gain_ref
  1.9 1.3 reshape.40.gain_ref
  3.2 0.0 copy-done
  3.2 1.3 pad.4.tab_ref
  4.5 1.0 copy.23.seg_ref
  5.5 52.0 %exchange_project.1 = (bf16[2,512,768]{2,1,0:T(8,128)(2,1)}, bf16[2,512,768]{2,1,0:T(8,128)(2,1)}, f32[2,8,128]{2,1,0:T(8,128)}, bf16[1024,768]{1,0:T(8,128)(2,1...) custom-call(bf16[2,512,768]{2,1,0:T(8,128)(2,1)} %x_ref.1, ...), custom_call_target="tpu_custom_call" | custom-call | tf_op jit(solution)/shard_map/exchange_project/pallas_call | solution.py:1179
  57.6 25.5 %attention_forward.1 = (bf16[1024,768]{1,0:T(8,128)(2,1)}, f32[1024,768]{1,0:T(8,128)}, bf16[6,1024,128]{2,1,0:T(8,128)(2,1)}) custom-call(bf16[1024,768]{1,0:T(8,128)(2,1)} %get-tuple-element.40.q_ref, bf16[1024,768]{1,0:T(8,128)(2,1)} %get-tuple-element.41.k_ref, bf16[1024,768]{1,0:T(8,128)(2,1)} %get-tuple-element.42.v_ref, s32[1024,1]{1,0:T(8,128)} %copy.23.seg_ref, ...), custom_call_target="tpu_custom_call" | custom-call | tf_op jit(solution)/shard_map/attention_forward/pallas_call | solution.py:1179
  83.1 141.4 %feed_forward.1 = (f32[2,512,768]{2,1,0:T(8,128)}, f32[1024,768]{1,0:T(8,128)}, bf16[1024,768]{1,0:T(8,128)(2,1)}, f32[1,768]{1,0:T(1,128)}, f32[48,384]{1,0:T(8...) custom-call(bf16[1024,768]{1,0:T(8,128)(2,1)} %bitcast.12, bf16[1024,768]{1,0:T(8,128)(2,1)} %get-tuple-element.44.ctx_ref, ...), custom_call_target="tpu_custom_call" | custom-call | tf_op jit(solution)/shard_map/feed_forward/pallas_call | solution.py:1179
  224.5 41.8 %attention_backward.1 = (bf16[1024,768]{1,0:T(8,128)(2,1)}, bf16[1024,768]{1,0:T(8,128)(2,1)}, bf16[1024,768]{1,0:T(8,128)(2,1)}, f32[16,128]{1,0:T(8,128)}) custom-call(bf16[1024,768]{1,0:T(8,128)(2,1)} %get-tuple-element.40.q_ref, bf16[1024,768]{1,0:T(8,128)(2,1)} %get-tuple-element.41.k_ref, bf16[1024,768]{1,0:T(8,128)(2,1)} %get-tuple-element.42.v_ref, ...), custom_call_target="tpu_custom_call" | custom-call | tf_op jit(solution)/shard_map/attention_backward/pallas_call | solution.py:1179
  266.3 60.8 %projection_gradients.1 = (f32[2,512,768]{2,1,0:T(8,128)}, f32[48,384]{1,0:T(8,128)}, f32[48,384]{1,0:T(8,128)}, f32[48,384]{1,0:T(8,128)}, f32[8,1024]{1,0:T(8,128)}) custom-call(bf16[1024,768]{1,0:T(8,128)(2,1)} %bitcast.13, f32[1024,768]{1,0:T(8,128)} %get-tuple-element.47.gm_ref, bf16[1024,768]{1,0:T(8,128)(2,1)} %get-tuple-element.51.dq_ref, ...), custom_call_target="tpu_custom_call" | custom-call | tf_op jit(solution)/shard_map/projection_gradients/pallas_call | solution.py:1179
  327.1 1.4 slice_reduce_fusion
  328.5 0.7 slice_bitcast_fusion.1
  329.2 0.6 slice_bitcast_fusion
  329.8 0.0 copy-start.1
  329.8 3.9 %copy.33 = f32[2,512,768]{2,1,0:T(8,128)} copy(f32[2,512,768]{2,1,0:T(8,128)} %get-tuple-element.82) | data formatting | bytes 6291456
  333.7 0.0 copy-done.1
  333.7 0.0 copy-start.7
  333.7 0.0 copy-start.6
  333.7 0.0 copy-start.5
  333.7 0.0 copy-start.4
  333.7 0.0 copy-start.3
  333.7 0.0 copy-start.2
  333.8 1.7 copy.34
  335.4 0.0 copy-done.7
  335.4 0.6 copy.35
  336.1 0.0 copy-done.6
  336.1 0.6 copy.36
  336.7 0.0 copy-done.5
  336.7 0.6 copy.37
  337.3 0.0 copy-done.4
  337.3 0.6 copy.38
  338.0 0.0 copy-done.3
  338.0 0.7 copy.39
  338.7 0.0 copy-done.2
  338.7 0.7 copy.40
  (2 shorter events, 0.0 us)
Async XLA Ops:
  0.6 2.6 copy-start
  329.8 3.9 %copy-start.1 = (f32[2,512,768]{2,1,0:T(8,128)S(1)}, f32[2,512,768]{2,1,0:T(8,128)}, u32[]{:S(2)}) copy-start(f32[2,512,768]{2,1,0:T(8,128)} %get-tuple-element.83) | copy-start | bytes 9437188
  333.7 1.7 copy-start.7
  333.7 2.3 copy-start.6
  333.7 3.0 copy-start.5
  333.7 3.6 %copy-start.4 = (f32[48,384]{1,0:T(8,128)S(1)}, f32[48,384]{1,0:T(8,128)}, u32[]{:S(2)}) copy-start(f32[48,384]{1,0:T(8,128)} %get-tuple-element.89) | copy-start | bytes 221188
  333.7 4.2 %copy-start.3 = (f32[48,1536]{1,0:T(8,128)S(1)}, f32[48,1536]{1,0:T(8,128)}, u32[]{:S(2)}) copy-start(f32[48,1536]{1,0:T(8,128)} %get-tuple-element.90) | copy-start | bytes 884740
  333.7 4.9 %copy-start.2 = (f32[48,1536]{1,0:T(8,128)S(1)}, f32[48,1536]{1,0:T(8,128)}, u32[]{:S(2)}) copy-start(f32[48,1536]{1,0:T(8,128)} %get-tuple-element.91) | copy-start | bytes 884740

commit v2 on v1

v2 whole, which is shorter than its diff:
```python
import functools

import jax
import jax.numpy as jnp
from jax import lax
from jax.experimental import pallas as pl
from jax.experimental.pallas import tpu as pltpu
from jax.sharding import PartitionSpec as P

MESH = pl.DeviceIdType.MESH
BF = jnp.bfloat16
F32 = jnp.float32
HIGHEST = lax.Precision.HIGHEST
EPSILON = 1e-06
THRESHOLDS = (12, 16, 23, 32, 46, 64, 91)
MASK_OUT = -float(2**30)
DH = 64
SPAN = 512
LANES = 128
VMEM_BYTES = 62 * 2**20


def nn(left, right):
    return lax.dot_general(left, right, (((1,), (0,)), ((), ())), preferred_element_type=F32)


def nt(left, right):
    return lax.dot_general(left, right, (((1,), (1,)), ((), ())), preferred_element_type=F32)


def tn(left, right):
    return lax.dot_general(left, right, (((0,), (0,)), ((), ())), preferred_element_type=F32)


def iota(shape, dim):
    return lax.broadcasted_iota(jnp.int32, shape, dim)


def bucket_ids(offsets):
    distance = jnp.abs(offsets)
    far_ids = 8 + sum((distance >= threshold).astype(jnp.int32) for threshold in THRESHOLDS)
    return jnp.where(offsets > 0, 16, 0) + jnp.where(distance < 8, distance, far_ids)


def rms_scale(values):
    return lax.rsqrt(jnp.mean(values * values, -1, keepdims=True) + EPSILON)


def rms_back(grad_normed, normed, scale, gain):
    scaled = grad_normed * gain
    return scale * (scaled - normed * jnp.mean(scaled * normed, -1, keepdims=True))


def gelu_pair(v):
    square = v * v
    half = 0.5 + 0.5 * jnp.tanh(v * (0.7978845608028654 + 0.035677408136300125 * square))
    slope = half + v * half * (1.0 - half) * (1.5957691216057308 + 0.2140644488178007 * square)
    return v * half, slope


class Place:
    def __init__(self, depth):
        d, t = lax.axis_index("dp"), lax.axis_index("tensor")
        self.t = t
        self.z, self.y, self.c = lax.div(d, 4), lax.rem(lax.div(d, 2), 2), lax.rem(d, 2)
        self.depth = depth
        self.sib = (d + 1 - 2 * self.c, t)
        self.ypeer = (d + 2 - 4 * self.y, t)
        self.xpeer = (d, 1 - t)
        rest = lax.rem(d, 4)
        self.zs = [lax.rem(self.z + step, depth) for step in range(1, depth)]
        self.zpeers = [(z * 4 + rest, t) for z in self.zs]

    def barrier(self):
        semaphore = pltpu.get_barrier_semaphore()
        peers = [self.sib, self.ypeer, self.xpeer] + self.zpeers
        for peer in peers:
            pl.semaphore_signal(semaphore, inc=1, device_id=peer, device_id_type=MESH)
        pl.semaphore_wait(semaphore, len(peers))


class Copy:
    def __init__(self, **parts):
        self.parts = parts

    def made(self):
        return pltpu.make_async_remote_copy(device_id_type=MESH, **self.parts)

    def start(self):
        self.made().start()

    def wait_recv(self):
        self.made().wait_recv()

    def wait_send(self):
        self.made().wait_send()


def local(src, dst, sem):
    return pltpu.make_async_copy(src, dst, sem)


def remote(src, dst, sems, index, peer):
    send, recv = sems
    return Copy(
        src_ref=src, dst_ref=dst, send_sem=send.at[index], recv_sem=recv.at[index], device_id=peer
    )


class Gather:
    def __init__(self, place, ref, width, sems, item, x_first):
        self.p, self.ref, self.width, self.sems, self.item = place, ref, width, sems, item
        self.x_first = x_first
        self.first, self.second = (
            (place.xpeer, place.ypeer) if x_first else (place.ypeer, place.xpeer)
        )

    def cols(self, x):
        return pl.ds(pl.multiple_of(x * self.width, LANES), self.width)

    def region(self, y, x):
        return self.ref.at[:, y, self.p.c, :, self.cols(x)]

    def send(self, index, src, peer):
        return remote(src, src, self.sems, (self.item, index), peer)

    def copies(self):
        p = self.p
        own = self.ref.at[p.z, p.y, p.c, :, self.cols(p.t)]
        regions = [self.region(p.y, p.t)]
        regions.append(self.region(p.y, 1 - p.t) if self.x_first else self.region(1 - p.y, p.t))
        regions.append(self.region(1 - p.y, p.t) if self.x_first else self.region(p.y, 1 - p.t))
        regions.append(self.region(1 - p.y, 1 - p.t))
        n = len(p.zpeers)
        zs = [self.send(i, own, peer) for i, peer in enumerate(p.zpeers)]
        first = self.send(n, regions[0], self.first)
        seconds = [self.send(n + 1 + i, regions[i], self.second) for i in range(2)]
        sibs = [self.send(n + 3 + i, regions[i], p.sib) for i in range(4)]
        return zs, first, seconds, sibs

    def start(self):
        for copy in self.copies()[0]:
            copy.start()

    def step1(self):
        zs, first, seconds, sibs = self.copies()
        for copy in zs:
            copy.wait_recv()
        first.start()
        seconds[0].start()
        sibs[0].start()

    def step2(self):
        _, first, seconds, sibs = self.copies()
        first.wait_recv()
        seconds[1].start()
        sibs[1].start()

    def step3(self):
        _, _, seconds, sibs = self.copies()
        seconds[0].wait_recv()
        sibs[2].start()
        seconds[1].wait_recv()
        sibs[3].start()

    def finish(self):
        zs, first, seconds, sibs = self.copies()
        for copy in sibs:
            copy.wait_recv()
        for copy in zs + [first] + seconds + sibs:
            copy.wait_send()


class GatherX(Gather):
    def copies(self):
        p = self.p
        n = len(p.zpeers)
        own = self.ref.at[p.z, p.y, p.c, :, self.cols(p.t)]
        other = self.ref.at[p.z, p.y, p.c, :, self.cols(1 - p.t)]
        regions = [self.region(y, x) for y in (p.y, 1 - p.y) for x in (p.t, 1 - p.t)]
        first = self.send(0, own, p.xpeer)
        zs = [
            [self.send(1 + side * n + i, block, peer) for i, peer in enumerate(p.zpeers)]
            for side, block in enumerate((own, other))
        ]
        lasts = [self.send(1 + 2 * n + i, regions[i], p.ypeer) for i in range(2)]
        sibs = [self.send(3 + 2 * n + i, regions[i], p.sib) for i in range(4)]
        return first, zs, lasts, sibs

    def start(self):
        first, zs, _, _ = self.copies()
        first.start()
        for copy in zs[0]:
            copy.start()

    def step1(self):
        first, zs, _, _ = self.copies()
        first.wait_recv()
        for copy in zs[1]:
            copy.start()

    def step2(self, side):
        _, zs, lasts, sibs = self.copies()
        for copy in zs[side]:
            copy.wait_recv()
        lasts[side].start()
        sibs[side].start()

    def step3(self):
        _, _, lasts, sibs = self.copies()
        for side in range(2):
            lasts[side].wait_recv()
            sibs[2 + side].start()

    def finish(self):
        first, zs, lasts, sibs = self.copies()
        for copy in sibs:
            copy.wait_recv()
        for copy in [first] + zs[0] + zs[1] + lasts + sibs:
            copy.wait_send()


def gather_sems(items, depth):
    return [pltpu.SemaphoreType.DMA((items, depth + 6))] * 2


class Scatter:
    def __init__(self, place, ref, width, bufs, sems, item, y_first):
        self.p, self.ref, self.width, self.sems, self.item = place, ref, width, sems, item
        self.r0, self.r1, self.r2, self.r3 = bufs
        self.y_first = y_first

    def cols(self, x):
        return pl.ds(pl.multiple_of(x * self.width, LANES), self.width)

    def copies(self):
        p, ref = self.p, self.ref
        sib = remote(ref.at[:, :, 1 - p.c], self.r0, self.sems, (self.item, 0), p.sib)
        if self.y_first:
            half = remote(ref.at[:, 1 - p.y, p.c], self.r1, self.sems, (self.item, 1), p.ypeer)
            quarter = remote(
                ref.at[:, p.y, p.c, :, self.cols(1 - p.t)],
                self.r2,
                self.sems,
                (self.item, 2),
                p.xpeer,
            )
        else:
            half = remote(
                ref.at[:, :, p.c, :, self.cols(1 - p.t)],
                self.r1,
                self.sems,
                (self.item, 1),
                p.xpeer,
            )
            quarter = remote(
                ref.at[:, 1 - p.y, p.c, :, self.cols(p.t)],
                self.r2,
                self.sems,
                (self.item, 2),
                p.ypeer,
            )
        zs = [
            remote(
                ref.at[z, p.y, p.c, :, self.cols(p.t)],
                self.r3.at[i],
                self.sems,
                (self.item, 3 + i),
                peer,
            )
            for i, (z, peer) in enumerate(zip(p.zs, p.zpeers))
        ]
        return sib, half, quarter, zs

    def step0(self):
        self.copies()[0].start()

    def step1(self):
        p = self.p
        sib, half, _, _ = self.copies()
        sib.wait_recv()
        kept = self.ref.at[:, :, p.c]
        kept[...] = (kept[...].astype(F32) + self.r0[...].astype(F32)).astype(BF)
        half.start()

    def step2(self):
        p = self.p
        _, half, quarter, _ = self.copies()
        half.wait_recv()
        if self.y_first:
            kept = self.ref.at[:, p.y, p.c]
        else:
            kept = self.ref.at[:, :, p.c, :, self.cols(p.t)]
        kept[...] = (kept[...].astype(F32) + self.r1[...].astype(F32)).astype(BF)
        quarter.start()

    def step3(self):
        p = self.p
        _, _, quarter, zs = self.copies()
        quarter.wait_recv()
        kept = self.ref.at[:, p.y, p.c, :, self.cols(p.t)]
        kept[...] = (kept[...].astype(F32) + self.r2[...].astype(F32)).astype(BF)
        for copy in zs:
            copy.start()

    def finish(self, out, offset):
        p = self.p
        sib, half, quarter, zs = self.copies()
        for copy in zs:
            copy.wait_recv()
        total = self.ref[p.z, p.y, p.c, :, self.cols(p.t)].astype(F32)
        for i in range(len(zs)):
            total = total + self.r3[i].astype(F32)
        out[:, pl.ds(pl.multiple_of(offset, LANES), self.width)] = total
        for copy in [sib, half, quarter] + zs:
            copy.wait_send()


def scatter_bufs(items, depth, rows, width, y_first):
    lead = () if items is None else (items,)
    return [
        pltpu.VMEM(lead + (depth, 2, rows, 2 * width), BF),
        pltpu.VMEM(lead + ((depth, rows, 2 * width) if y_first else (depth, 2, rows, width)), BF),
        pltpu.VMEM(lead + (depth, rows, width), BF),
        pltpu.VMEM(lead + (depth - 1, rows, width), BF),
    ]


def scatter_sems(items, depth):
    return [pltpu.SemaphoreType.DMA((items, depth + 2))] * 2


def flat(values):
    if len(values.shape) == 2:
        return values
    return values.reshape(-1, values.shape[-1])


def project_rows(x_rows, gain):
    rows = x_rows.astype(F32)
    return (rows * rms_scale(rows) * gain).astype(BF)


def project(low_ref, w_ref, out_ref):
    weight = flat(w_ref[...])
    half = low_ref.shape[0] // 2

    def one(i, carry):
        rows = pl.ds(pl.multiple_of(i * half, half), half)
        out_ref[rows, :] = nn(low_ref[rows, :], weight).astype(BF)
        return carry

    lax.fori_loop(0, 2, one, 0)


def k1_plain(x_ref, gain_ref, wq_ref, wk_ref, wv_ref, q_ref, k_ref, v_ref, low_ref):
    low_ref[...] = project_rows(x_ref[...], gain_ref[...])
    for weight, out in ((wq_ref, q_ref), (wk_ref, k_ref), (wv_ref, v_ref)):
        project(low_ref, weight, out)


def bias_rows(tabs_ref, out_ref, flipped):
    offsets = iota((LANES, 4 * LANES), 1) - 2 * LANES
    onehot = (bucket_ids(-offsets if flipped else offsets) == iota((LANES, 4 * LANES), 0)).astype(F32)
    for half in range(2):
        out_ref[half * 8 : half * 8 + 8, :] = jnp.dot(
            tabs_ref[half], onehot, precision=HIGHEST, preferred_element_type=F32
        )


def head_row(pair, per_half):
    return 8 * lax.div(pair, per_half) + 2 * lax.rem(pair, per_half)


def bias_strip(row):
    spread = jnp.broadcast_to(row, (LANES, 4 * LANES))
    return pltpu.roll(spread, 3 * LANES, 1, stride=1, stride_axis=0)


def window(tile, rows, length):
    reach = -(-SPAN // rows)
    return max(0, (tile - reach) * rows), min(length, (tile + reach + 1) * rows)


def segment_lanes(seg_ref):
    onehot = seg_ref[...] == iota((seg_ref.shape[0], LANES), 1)
    inside = iota((seg_ref.shape[0], LANES), 1) < 16
    return onehot, inside


def pair_cols(pair):
    return pl.ds(pl.multiple_of(pair * LANES, LANES), LANES)


def spread3(value):
    top = value.astype(BF).astype(F32)
    mid = (value - top).astype(BF).astype(F32)
    return top, mid, value - top - mid


TILE = 256
NEAR = SPAN // LANES


def key_lanes(seg_ref):
    onehot, inside = segment_lanes(seg_ref)
    return jnp.where(onehot, 0.0, jnp.where(inside, 1.0, 0.0)).astype(BF)


def fwd_setup(seg_ref, tabs_ref, bias_ref, segq_ref, segk_ref):
    bias_rows(tabs_ref, bias_ref, False)
    onehot, _ = segment_lanes(seg_ref)
    segq_ref[...] = jnp.where(onehot, MASK_OUT, 0.0).astype(BF)
    segk_ref[...] = key_lanes(seg_ref)


def fwd_pair(pair, q_ref, k_ref, v_ref, ctx_ref, feat_ref, bias_ref, segq_ref, segk_ref):
    length, width = q_ref.shape
    per_half = width // LANES // 2
    tile, near = TILE, NEAR
    cols = pair_cols(pair)
    row = head_row(pair, per_half)
    lane = iota((tile, LANES), 1)
    low_half = lane < DH
    strips, fars = [], []
    for hh in range(2):
        line = bias_ref[pl.ds(row + hh, 1), :]
        strips.append(bias_strip(line))
        fars.append((line[:, 0:1], line[:, 4 * LANES - 1 : 4 * LANES]))
    for index in range(length // tile):
        rows = slice(index * tile, (index + 1) * tile)
        start, stop = window(index, tile, length)
        queries = q_ref[rows, cols]
        zero = jnp.zeros_like(queries)
        q_feat = segq_ref[rows, :]
        left = jnp.concatenate(
            [
                jnp.concatenate([jnp.where(low_half, queries, zero), q_feat], 1),
                jnp.concatenate([jnp.where(low_half, zero, queries), q_feat], 1),
            ],
            0,
        )
        right = jnp.concatenate([k_ref[start:stop, cols], segk_ref[start:stop, :]], 1)
        scores = nt(left, right)
        weights, peaks = [], []
        for hh in range(2):
            for part in range(tile // LANES):
                at = hh * tile + part * LANES
                q_block = index * (tile // LANES) + part
                blocks = []
                for k_block in range(start // LANES, stop // LANES):
                    delta = k_block - q_block
                    if abs(delta) > near:
                        blocks.append(None)
                        continue
                    col = k_block * LANES - start
                    block = scores[at : at + LANES, col : col + LANES]
                    if abs(delta) <= 1:
                        block = block + strips[hh][:, (delta + 1) * LANES : (delta + 2) * LANES]
                    else:
                        block = block + fars[hh][0 if delta < 0 else 1]
                    blocks.append(block)
                real = [block for block in blocks if block is not None]
                peak = functools.reduce(jnp.maximum, real)
                peak = jnp.max(peak, -1, keepdims=True)
                peaks.append(peak)
                weights.append(
                    jnp.concatenate(
                        [
                            jnp.zeros((LANES, LANES), BF)
                            if block is None
                            else jnp.exp(block - peak).astype(BF)
                            for block in blocks
                        ],
                        1,
                    )
                )
        values = v_ref[start:stop, cols]
        gathered = nn(
            jnp.concatenate(weights, 0), jnp.concatenate([values, jnp.ones_like(values)], 1)
        )
        normal = gathered[:, :LANES] / gathered[:, LANES:]
        context = jnp.where(low_half, normal[:tile], normal[tile:])
        ctx_ref[rows, cols] = context.astype(BF)
        logs = jnp.concatenate(peaks, 0) + jnp.log(gathered[:, LANES:])
        feature = q_feat.astype(F32)
        for hh in range(2):
            for i, piece in enumerate(spread3(logs[hh * tile : (hh + 1) * tile])):
                feature = jnp.where(lane == 16 + 3 * hh + i, -piece, feature)
        feat_ref[pair, rows, :] = feature.astype(BF)


def fwd_kernel(
    q_ref, k_ref, v_ref, seg_ref, tabs_ref, ctx_ref, feat_ref, bias_ref, segq_ref, segk_ref
):
    fwd_setup(seg_ref, tabs_ref, bias_ref, segq_ref, segk_ref)

    def one_pair(pair, carry):
        fwd_pair(pair, q_ref, k_ref, v_ref, ctx_ref, feat_ref, bias_ref, segq_ref, segk_ref)
        return carry

    lax.fori_loop(0, q_ref.shape[1] // LANES, one_pair, 0)


def bwd_setup(seg_ref, tabs_ref, bias_ref, sums_ref, far_ref, segk_ref, blockof_ref):
    length = seg_ref.shape[0]
    bias_rows(tabs_ref, bias_ref, True)
    sums_ref[...] = jnp.zeros_like(sums_ref)
    far_ref[...] = jnp.zeros_like(far_ref)
    segk_ref[...] = key_lanes(seg_ref)
    blockof_ref[...] = (
        lax.div(iota((length, LANES), 0), LANES) == iota((length, LANES), 1)
    ).astype(BF)


def bwd_pair(
    pair,
    q_ref,
    k_ref,
    v_ref,
    go_ref,
    ctx_ref,
    feat_ref,
    dq_ref,
    dk_ref,
    dv_ref,
    bias_ref,
    sums_ref,
    far_ref,
    segk_ref,
    blockof_ref,
    gofeat_ref,
    near_ref,
    acc_ref,
):
    length, width = q_ref.shape
    per_half = width // LANES // 2
    tile, near = TILE, NEAR
    flip = (iota((LANES, LANES), 0) + iota((LANES, LANES), 1) == LANES - 1).astype(F32)
    cols = pair_cols(pair)
    row = head_row(pair, per_half)
    lane = iota((tile, LANES), 1)
    low_half = lane < DH
    strips, fars = [], []
    for hh in range(2):
        line = bias_ref[pl.ds(row + hh, 1), :]
        strips.append(bias_strip(line))
        fars.append((line[:, 0:1], line[:, 4 * LANES - 1 : 4 * LANES]))
    grads_all = go_ref[:, cols]
    product = grads_all.astype(F32) * ctx_ref[:, cols].astype(F32)
    lane_all = iota((length, LANES), 1)
    feature = jnp.zeros((length, LANES), F32)
    for hh in range(2):
        keep = (lane_all < DH) if hh == 0 else (lane_all >= DH)
        total = jnp.sum(jnp.where(keep, product, 0.0), -1, keepdims=True)
        for i, piece in enumerate(spread3(total)):
            feature = jnp.where(lane_all == 3 * hh + i, -piece, feature)
    gofeat_ref[...] = feature.astype(BF)
    near_ref[...] = jnp.zeros_like(near_ref)
    acc_ref[...] = jnp.zeros_like(acc_ref)
    far_sums = [[jnp.zeros((1, LANES), F32) for _ in range(2)] for _ in range(2)]
    lane_row = iota((1, LANES), 1)
    for index in range(length // tile):
        rows = slice(index * tile, (index + 1) * tile)
        start, stop = window(index, tile, length)
        keys, values = k_ref[rows, cols], v_ref[rows, cols]
        zero = jnp.zeros_like(keys)
        seg_feat = segk_ref[rows, :].astype(F32)

        def ones_at(base, first):
            return jnp.where((lane >= first) & (lane < first + 3), 1.0, base).astype(BF)

        masked_keys = jnp.concatenate(
            [jnp.where(low_half, keys, zero), jnp.where(low_half, zero, keys)], 0
        )
        masked_values = jnp.concatenate(
            [jnp.where(low_half, values, zero), jnp.where(low_half, zero, values)], 0
        )
        key_feats = jnp.concatenate([ones_at(seg_feat, 16), ones_at(seg_feat, 19)], 0)
        value_feats = jnp.concatenate([ones_at(0.0, 0), ones_at(0.0, 3)], 0)
        queries = q_ref[start:stop, cols]
        grads = go_ref[start:stop, cols]
        logits = nt(
            jnp.concatenate([masked_keys, key_feats], 1),
            jnp.concatenate([queries, feat_ref[pair, start:stop, :]], 1),
        )
        shifted = nt(
            jnp.concatenate([masked_values, value_feats], 1),
            jnp.concatenate([grads, gofeat_ref[start:stop, :]], 1),
        )
        probs_rows, score_rows = [], []
        for hh in range(2):
            for part in range(tile // LANES):
                at = hh * tile + part * LANES
                k_block = index * (tile // LANES) + part
                probs, score_grads = [], []
                for q_block in range(start // LANES, stop // LANES):
                    delta = k_block - q_block
                    if abs(delta) > near:
                        probs.append(jnp.zeros((LANES, LANES), BF))
                        score_grads.append(jnp.zeros((LANES, LANES), BF))
                        continue
                    col = q_block * LANES - start
                    block = logits[at : at + LANES, col : col + LANES]
                    place = (1 - delta) * LANES
                    if abs(delta) <= 1:
                        block = block + strips[hh][:, place : place + LANES]
                    else:
                        block = block + fars[hh][0 if delta > 0 else 1]
                    prob = jnp.exp(block)
                    grad = prob * shifted[at : at + LANES, col : col + LANES]
                    if abs(delta) <= 1:
                        near_ref[hh, :, place : place + LANES] += grad
                    probs.append(prob.astype(BF))
                    score_grads.append(grad.astype(BF))
                probs_rows.append(jnp.concatenate(probs, 1))
                score_rows.append(jnp.concatenate(score_grads, 1))
        probs_all = jnp.concatenate(probs_rows, 0)
        scores_all = jnp.concatenate(score_rows, 0)
        value_grad = nn(probs_all, grads)
        dv_ref[rows, cols] = jnp.where(low_half, value_grad[:tile], value_grad[tile:]).astype(BF)
        key_grad = nn(scores_all, jnp.concatenate([queries, blockof_ref[start:stop, :]], 1))
        dk_ref[rows, cols] = jnp.where(
            low_half, key_grad[:tile, :LANES], key_grad[tile:, :LANES]
        ).astype(BF)
        acc_ref[start:stop, :] += tn(scores_all, masked_keys)
        for hh in range(2):
            for part in range(tile // LANES):
                at = hh * tile + part * LANES
                k_block = index * (tile // LANES) + part
                line = jnp.sum(key_grad[at : at + LANES, LANES:], 0, keepdims=True)
                far_sums[hh][0] += jnp.where(lane_row <= k_block - 2, line, 0.0)
                far_sums[hh][1] += jnp.where(lane_row >= k_block + 2, line, 0.0)
    dq_ref[:, cols] = acc_ref[...].astype(BF)
    for hh in range(2):
        turned = jnp.dot(flip, near_ref[hh], precision=HIGHEST, preferred_element_type=F32)
        turned = jnp.concatenate([turned, jnp.zeros((LANES, LANES), F32)], 1)
        turned = pltpu.roll(turned, 1, 1, stride=1, stride_axis=0)
        sums_ref[pl.ds(row + hh, 1), :] = jnp.sum(turned, 0, keepdims=True)
        last = lane_row == 0
        positive = jnp.sum(far_sums[hh][0], -1, keepdims=True)
        negative = jnp.sum(far_sums[hh][1], -1, keepdims=True)
        far_ref[pl.ds(row + hh, 1), :] = jnp.where(last, positive, jnp.where(lane_row == 1, negative, 0.0))


def bwd_table(tabg_ref, sums_ref, far_ref):
    offsets = 2 * LANES - iota((LANES, 4 * LANES), 1)
    onehot_buckets = (bucket_ids(offsets) == iota((LANES, 4 * LANES), 0)).astype(F32)
    table = lax.dot_general(
        sums_ref[...],
        onehot_buckets,
        (((1,), (1,)), ((), ())),
        precision=HIGHEST,
        preferred_element_type=F32,
    )
    lane = iota(tabg_ref.shape, 1)
    far = far_ref[...]
    table = table + jnp.where(lane == 31, far[:, 0:1], 0.0) + jnp.where(lane == 15, far[:, 1:2], 0.0)
    tabg_ref[...] = table


def bwd_kernel(
    q_ref,
    k_ref,
    v_ref,
    go_ref,
    ctx_ref,
    feat_ref,
    seg_ref,
    tabs_ref,
    dq_ref,
    dk_ref,
    dv_ref,
    tabg_ref,
    bias_ref,
    sums_ref,
    far_ref,
    segk_ref,
    blockof_ref,
    gofeat_ref,
    near_ref,
    acc_ref,
):
    bwd_setup(seg_ref, tabs_ref, bias_ref, sums_ref, far_ref, segk_ref, blockof_ref)

    def one_pair(pair, carry):
        bwd_pair(
            pair,
            q_ref,
            k_ref,
            v_ref,
            go_ref,
            ctx_ref,
            feat_ref,
            dq_ref,
            dk_ref,
            dv_ref,
            bias_ref,
            sums_ref,
            far_ref,
            segk_ref,
            blockof_ref,
            gofeat_ref,
            near_ref,
            acc_ref,
        )
        return carry

    lax.fori_loop(0, q_ref.shape[1] // LANES, one_pair, 0)
    bwd_table(tabg_ref, sums_ref, far_ref)


def k3_before(xs_ref, ctx_ref, wo, gain, middle_ref, ffn_ref, ffnt_ref):
    step = 256

    def one(i, carry):
        rows = pl.ds(pl.multiple_of(i * step, step), step)
        middle = xs_ref[rows, :].astype(F32) + nt(ctx_ref[rows, :], wo)
        middle_ref[rows, :] = middle
        low = (middle * rms_scale(middle) * gain).astype(BF)
        ffn_ref[rows, :] = low
        ffnt_ref[:, rows] = low.T
        return carry

    lax.fori_loop(0, middle_ref.shape[0] // step, one, 0)


def transpose_rows(src_ref, dst_ref):
    step = 256

    def one(i, carry):
        rows = pl.ds(pl.multiple_of(i * step, step), step)
        dst_ref[:, rows] = src_ref[rows, :].T
        return carry

    lax.fori_loop(0, src_ref.shape[0] // step, one, 0)


def ffn_rows(i, half, w_in, w_back, first, ffn_ref, cot_ref, hid_ref, gp_ref, up_ref, down_ref):
    rows = pl.ds(pl.multiple_of(i * half, half), half)
    hidden, slope = gelu_pair(nn(ffn_ref[rows, :], w_in))
    hidden = hidden.astype(BF)
    hid_ref[rows, :] = hidden
    grad_pre = (nn(cot_ref[rows, :], w_back) * slope).astype(BF)
    gp_ref[rows, :] = grad_pre
    up = nt(hidden, w_back)
    down = nt(grad_pre, w_in)

    @pl.when(first)
    def _():
        up_ref[rows, :] = up
        down_ref[rows, :] = down

    @pl.when(jnp.logical_not(first))
    def _():
        up_ref[rows, :] += up
        down_ref[rows, :] += down


def after_rows(rows, cot, up_ref, down_ref, gain, gain_ref, gm_ref, ca_ref, cat_ref):
    middle = gm_ref[rows, :]
    scale = rms_scale(middle)
    normed = middle * scale
    down = down_ref[rows, :]
    gain_ref[...] += jnp.sum(down * normed, 0, keepdims=True)
    grad = cot + rms_back(down, normed, scale, gain)
    gm_ref[rows, :] = grad
    low = grad.astype(BF)
    ca_ref[rows, :] = low
    cat_ref[:, rows] = low.T
    return middle + up_ref[rows, :]


def context_grad(ca_ref, wo, go_ref):
    step = 256

    def one(i, carry):
        rows = pl.ds(pl.multiple_of(i * step, step), step)
        go_ref[rows, :] = nn(ca_ref[rows, :], wo).astype(BF)
        return carry

    lax.fori_loop(0, ca_ref.shape[0] // step, one, 0)


def k3_plain(
    xs_ref,
    ctx_ref,
    cot_ref,
    gain_ref,
    wo_ref,
    wi_ref,
    wb_ref,
    out_ref,
    gm_ref,
    go_ref,
    ggain_ref,
    gwo_ref,
    gwi_ref,
    gwb_ref,
    ffn_ref,
    ffnt_ref,
    cott_ref,
    cotb_ref,
    hid_ref,
    gp_ref,
    up_ref,
    down_ref,
):
    length = ctx_ref.shape[0]
    half_rows = length // 2
    chunk = hid_ref.shape[1]
    gain = gain_ref[...]
    cotb_ref[...] = cot_ref[...].astype(BF)
    k3_before(xs_ref, ctx_ref, wo_ref[...], gain, gm_ref, ffn_ref, ffnt_ref)
    transpose_rows(cotb_ref, cott_ref)

    def one_chunk(k, carry):
        cols = pl.ds(pl.multiple_of(k * chunk, LANES), chunk)
        w_in, w_back = wi_ref[:, cols], wb_ref[:, cols]
        for i in range(2):
            ffn_rows(
                i, half_rows, w_in, w_back, k == 0, ffn_ref, cotb_ref, hid_ref, gp_ref, up_ref, down_ref
            )
        gwb_ref[:, cols] = nn(cott_ref[...], hid_ref[...]).astype(BF)
        gwi_ref[:, cols] = nn(ffnt_ref[...], gp_ref[...]).astype(BF)
        return carry

    lax.fori_loop(0, wi_ref.shape[1] // chunk, one_chunk, 0)
    ggain_ref[...] = jnp.zeros_like(ggain_ref)
    step = 256

    def finish_rows(i, carry):
        rows = pl.ds(pl.multiple_of(i * step, step), step)
        out_ref[rows, :] = after_rows(
            rows,
            cot_ref[rows, :],
            up_ref,
            down_ref,
            gain,
            ggain_ref,
            gm_ref,
            ffn_ref,
            cott_ref,
        )
        return carry

    lax.fori_loop(0, length // step, finish_rows, 0)
    context_grad(ffn_ref, wo_ref[...], go_ref)
    gwo_ref[...] = nn(cott_ref[...], ctx_ref[...]).astype(BF)


def low_transposed(xs_ref, gain, lowt_ref):
    step = 256

    def one(i, carry):
        rows = pl.ds(pl.multiple_of(i * step, step), step)
        lowt_ref[:, rows] = project_rows(xs_ref[rows, :], gain).T
        return carry

    lax.fori_loop(0, xs_ref.shape[0] // step, one, 0)


def input_rows(rows, xs_ref, gm_ref, grads, weights, gain, gain_out):
    down = sum(nt(grad[rows, :], flat(weight[...])) for grad, weight in zip(grads, weights))
    inputs = xs_ref[rows, :].astype(F32)
    scale = rms_scale(inputs)
    normed = inputs * scale
    gain_out[...] += jnp.sum(down * normed, 0, keepdims=True)
    return gm_ref[rows, :] + rms_back(down, normed, scale, gain)


def k5_plain(
    xs_ref,
    gm_ref,
    dq_ref,
    dk_ref,
    dv_ref,
    wq_ref,
    wk_ref,
    wv_ref,
    gain_ref,
    ig_ref,
    gwq_ref,
    gwk_ref,
    gwv_ref,
    again_ref,
    lowt_ref,
):
    gain = gain_ref[...]
    low_transposed(xs_ref, gain, lowt_ref)
    grads, weights = (dq_ref, dk_ref, dv_ref), (wq_ref, wk_ref, wv_ref)
    for grad, out in zip(grads, (gwq_ref, gwk_ref, gwv_ref)):
        out[...] = nn(lowt_ref[...], grad[...]).astype(BF)
    again_ref[...] = jnp.zeros_like(again_ref)
    step = 256

    def one(i, carry):
        rows = pl.ds(pl.multiple_of(i * step, step), step)
        ig_ref[rows, :] = input_rows(rows, xs_ref, gm_ref, grads, weights, gain, again_ref)
        return carry

    lax.fori_loop(0, xs_ref.shape[0] // step, one, 0)


def run_all(steps):
    for step in steps:
        step()


def at_step(index, plan):
    for number, steps in enumerate(plan):
        if steps:

            @pl.when(index == number)
            def _(steps=steps):
                run_all(steps)


def attend_fused(
    depth,
    x_ref,
    cot_ref,
    gain_ref,
    tab_ref,
    seg_ref,
    wq_shard,
    wk_shard,
    wv_shard,
    wo_shard,
    wi_shard,
    wb_shard,
    xs_out,
    coto_ref,
    tabs_ref,
    q_out,
    k_out,
    v_out,
    ctx_ref,
    feat_ref,
    wq_out,
    wk_out,
    wv_out,
    wo_out,
    wi_out,
    wb_out,
    xs_ref,
    cotf_ref,
    cotb_ref,
    q_ref,
    k_ref,
    v_ref,
    wq_ref,
    wk_ref,
    wv_ref,
    wo_ref,
    wi_ref,
    wb_ref,
    low_ref,
    bias_ref,
    segq_ref,
    segk_ref,
    r_send,
    r_recv,
    g_send,
    g_recv,
    x_send,
    x_recv,
    l_sem,
):
    p = Place(depth)
    half_rows = x_ref.shape[1]
    width = wq_shard.shape[1]
    early, part = wi_ref.shape[0], wi_ref.shape[-1] // 2
    x_sems, g_sems = (x_send, x_recv), (g_send, g_recv)
    weights = (wq_ref, wk_ref, wv_ref)
    heads = [GatherX(p, ref, width, (r_send, r_recv), i, True) for i, ref in enumerate(weights)]
    for item, shard in zip(heads, (wq_shard, wk_shard, wv_shard)):
        item.ref[p.z, p.y, p.c, :, item.cols(p.t)] = shard[...]
    cot_load = local(cot_ref.at[1 - p.t], cotf_ref, l_sem.at[0])
    cot_load.start()
    tabs_ref[p.t] = tab_ref[...]
    p.barrier()
    for item in heads:
        item.start()
    moves = [
        remote(x_ref.at[1 - p.t], xs_ref.at[p.t], x_sems, 0, p.xpeer),
        remote(tabs_ref.at[p.t], tabs_ref.at[p.t], x_sems, 1, p.xpeer),
        remote(cotb_ref, coto_ref, x_sems, 2, p.xpeer),
    ]
    moves[0].start()
    moves[1].start()
    xs_ref[p.t] = x_ref[p.t]
    out_item = Gather(p, wo_ref, width, g_sems, 0, True)
    out_item.ref[p.z, p.y, p.c, :, out_item.cols(p.t)] = wo_shard[...]
    chunks = []
    for k in range(early):
        pair = []
        for side, (ref, shard) in enumerate(((wi_ref, wi_shard), (wb_ref, wb_shard))):
            item = Gather(p, ref.at[k], part, g_sems, 1 + 2 * k + side, True)
            item.ref[p.z, p.y, p.c, :, item.cols(p.t)] = shard[:, k * part : (k + 1) * part]
            pair.append(item)
        chunks.append(pair)

    def chunk(k, name):
        return [getattr(item, name) for item in chunks[k]] if k < early else []

    def rows_of(half):
        return pl.ds(pl.multiple_of(half * half_rows, half_rows), half_rows)

    low_ref[rows_of(p.t), :] = project_rows(x_ref[p.t], gain_ref[...])
    for item in heads:
        item.step1()
    fwd_setup_early = moves[1].wait_recv
    for item in heads:
        item.step2(0)
        item.step2(1)
    out_item.start()
    cot_load.wait()
    cotb_ref[...] = cotf_ref[...].astype(BF)
    fwd_setup_early()
    fwd_setup(seg_ref, tabs_ref, bias_ref, segq_ref, segk_ref)
    moves[0].wait_recv()
    moves[2].start()
    low_ref[rows_of(1 - p.t), :] = project_rows(xs_ref[1 - p.t], gain_ref[...])
    saves = [local(xs_ref, xs_out, l_sem.at[1])]
    saves[0].start()
    heads[0].step3()
    heads[0].finish()
    project(low_ref, wq_ref, q_ref)
    heads[1].step3()
    run_all(chunk(0, "start"))
    heads[1].finish()
    project(low_ref, wk_ref, k_ref)
    heads[2].step3()
    out_item.step1()
    heads[2].finish()
    project(low_ref, wv_ref, v_ref)
    for i, (src, dst) in enumerate(
        zip((q_ref, k_ref, v_ref) + weights, (q_out, k_out, v_out, wq_out, wk_out, wv_out))
    ):
        saves.append(local(src, dst, l_sem.at[2 + i]))
        saves[-1].start()

    def save(src, dst, index):
        return lambda: local(src, dst, l_sem.at[index]).start()

    def save_chunk(k):
        if k >= early:
            return []
        return [
            save(wi_ref.at[k], wi_out.at[k], 9 + 2 * k),
            save(wb_ref.at[k], wb_out.at[k], 10 + 2 * k),
        ]

    plan = [
        chunk(0, "step1") + [out_item.step2] + chunk(1, "start"),
        chunk(0, "step2") + [out_item.step3] + chunk(1, "step1") + chunk(2, "start"),
        chunk(0, "step3") + chunk(1, "step2") + [out_item.finish, save(wo_ref, wo_out, 8)],
        chunk(0, "finish") + save_chunk(0) + chunk(1, "step3") + chunk(2, "step1"),
        chunk(1, "finish") + save_chunk(1) + chunk(2, "step2"),
        chunk(2, "step3"),
    ]

    def one_pair(pair, carry):
        at_step(pair, plan)
        fwd_pair(pair, q_ref, k_ref, v_ref, ctx_ref, feat_ref, bias_ref, segq_ref, segk_ref)
        return carry

    lax.fori_loop(0, q_ref.shape[1] // LANES, one_pair, 0)
    run_all(chunk(2, "finish") + save_chunk(2))
    moves[2].wait_recv()
    for move in moves:
        move.wait_send()
    for one in saves:
        one.wait()
    local(wo_ref, wo_out, l_sem.at[8]).wait()
    for k in range(early):
        local(wi_ref.at[k], wi_out.at[k], l_sem.at[9 + 2 * k]).wait()
        local(wb_ref.at[k], wb_out.at[k], l_sem.at[10 + 2 * k]).wait()


def ffn_fused(
    depth,
    early,
    here,
    xs_ref,
    ctx_ref,
    cot_ref,
    coto_ref,
    gain_ref,
    wo_ref,
    wi_in,
    wb_in,
    wi_shard,
    wb_shard,
    out_ref,
    gm_ref,
    go_ref,
    ggain_ref,
    gwo_ref,
    gwi_ref,
    gwb_ref,
    gi_out,
    gb_out,
    wi_ref,
    wb_ref,
    gout_ref,
    ffn_ref,
    ffnt_ref,
    cott_ref,
    cotf_ref,
    cotb_ref,
    hid_ref,
    gp_ref,
    up_ref,
    down_ref,
    obuf_ref,
    obuf2_ref,
    o0,
    o1,
    o2,
    o3,
    i0,
    i1,
    i2,
    i3,
    b0,
    b1,
    b2,
    b3,
    g_send,
    g_recv,
    s_send,
    s_recv,
    x_send,
    x_recv,
    l_sem,
):
    p = Place(depth)
    length = ctx_ref.shape[0]
    half_rows = length // 2
    chunks = wi_ref.shape[0]
    width = gwo_ref.shape[1]
    part = wi_ref.shape[-1] // 2
    g_sems, s_sems, x_sems = (g_send, g_recv), (s_send, s_recv), (x_send, x_recv)
    late = chunks - early

    def g_chunk(k):
        return (
            Gather(p, wi_ref.at[k], part, g_sems, 2 * (k - early), True),
            Gather(p, wb_ref.at[k], part, g_sems, 1 + 2 * (k - early), False),
        )

    def s_chunk(k):
        return (
            Scatter(
                p, wi_ref.at[k], part, [r.at[k] for r in (i0, i1, i2, i3)], s_sems, 1 + 2 * k, True
            ),
            Scatter(
                p, wb_ref.at[k], part, [r.at[k] for r in (b0, b1, b2, b3)], s_sems, 2 + 2 * k, False
            ),
        )

    def load_chunk(k):
        return (
            local(wi_in.at[k], wi_ref.at[k], l_sem.at[1 + 2 * k]),
            local(wb_in.at[k], wb_ref.at[k], l_sem.at[2 + 2 * k]),
        )

    def save_chunk(k):
        return (
            local(wi_ref.at[k], gi_out.at[k - here], l_sem.at[1 + 2 * k]),
            local(wb_ref.at[k], gb_out.at[k - here], l_sem.at[2 + 2 * k]),
        )

    def when_gather(k, name):
        @pl.when((k >= early) & (k < chunks))
        def _():
            for item in g_chunk(k):
                getattr(item, name)()

    def when_scatter(k, name):
        @pl.when((k >= 0) & (k < here))
        def _():
            for item, out in zip(s_chunk(k), (gwi_ref, gwb_ref)):
                if name == "finish":
                    item.finish(out, k * part)
                else:
                    getattr(item, name)()

    cot_load = local(cot_ref.at[p.t], cotf_ref, l_sem.at[0])
    cot_load.start()
    for k in range(early):
        for one in load_chunk(k):
            one.start()
    for k in range(early, chunks):
        for item, shard in zip(g_chunk(k), (wi_shard, wb_shard)):
            item.ref[p.z, p.y, p.c, :, item.cols(p.t)] = shard[:, k * part : (k + 1) * part]
    p.barrier()
    when_gather(early, "start")
    when_gather(early + 1, "start")
    gain = gain_ref[...]
    k3_before(xs_ref, ctx_ref, flat(wo_ref[...]), gain, gm_ref, ffn_ref, ffnt_ref)
    when_gather(early, "step1")
    cotb_ref[1 - p.t] = coto_ref[...]
    cot_load.wait()
    cotb_ref[p.t] = cotf_ref[...].astype(BF)
    cotb = cotb_ref.reshape(length, cotb_ref.shape[2])
    transpose_rows(cotb, cott_ref)
    when_gather(early, "step2")

    def one_chunk(k, carry):
        when_gather(k + early, "step3")
        when_gather(k + early + 1, "step1")
        when_gather(k + early + 2, "start")

        @pl.when(k < early)
        def _():
            for one in load_chunk(k):
                one.wait()

        @pl.when(k >= early)
        def _():
            for item in g_chunk(k):
                item.finish()

        when_scatter(k - 2, "step2")
        w_in, w_back = flat(wi_ref[k]), flat(wb_ref[k])
        args = (w_in, w_back, k == 0, ffn_ref, cotb, hid_ref, gp_ref, up_ref, down_ref)
        ffn_rows(0, half_rows, *args)
        when_scatter(k - 1, "step1")
        when_gather(k + early + 1, "step2")
        ffn_rows(1, half_rows, *args)
        when_scatter(k - 3, "step3")
        wb_ref[k] = nn(cott_ref[...], hid_ref[...]).astype(BF).reshape(wb_ref.shape[1:])
        when_scatter(k - 4, "finish")
        wi_ref[k] = nn(ffnt_ref[...], gp_ref[...]).astype(BF).reshape(wi_ref.shape[1:])
        when_scatter(k, "step0")

        @pl.when(k >= here)
        def _():
            for one in save_chunk(k):
                one.start()

        return carry

    lax.fori_loop(0, chunks, one_chunk, 0)
    ggain_ref[...] = jnp.zeros_like(ggain_ref)
    step = 256

    def finish_rows(own, i):
        half = p.t if own else 1 - p.t
        at = pl.ds(pl.multiple_of(i * step, step), step)
        rows = pl.ds(pl.multiple_of(half * half_rows + i * step, step), step)
        cot = cotf_ref[at, :] if own else cotb_ref[1 - p.t, at, :].astype(F32)
        out = after_rows(
            rows, cot, up_ref, down_ref, gain, ggain_ref, gm_ref, ffn_ref, cott_ref
        )
        if own:
            out_ref[p.t, at, :] = out
        else:
            obuf_ref[at, :] = out.astype(BF)

    for i in range(half_rows // step):
        finish_rows(False, i)
    out_move = remote(obuf_ref, obuf2_ref, x_sems, 0, p.xpeer)
    out_move.start()
    for stage, name in ((1, "step1"), (2, "step2"), (3, "step3"), (4, "finish")):
        for k in range(max(0, chunks - stage), here):
            when_scatter(k, name)
    for i in range(half_rows // step):
        finish_rows(True, i)
    gout_ref[...] = nn(cott_ref[...], ctx_ref[...]).astype(BF).reshape(gout_ref.shape)
    s_out = Scatter(p, gout_ref, width, (o0, o1, o2, o3), s_sems, 0, True)
    s_out.step0()
    context_grad(ffn_ref, flat(wo_ref[...]), go_ref)
    s_out.step1()
    s_out.step2()
    s_out.step3()
    out_move.wait_recv()
    out_ref[1 - p.t] = obuf2_ref[...].astype(F32)
    s_out.finish(gwo_ref, 0)
    out_move.wait_send()
    for k in range(here, chunks):
        for one in save_chunk(k):
            one.wait()


def back_fused(
    depth,
    q_in,
    k_in,
    v_in,
    go_ref,
    ctx_ref,
    feat_ref,
    seg_ref,
    tabs_ref,
    xs_in,
    gm_in,
    wq_in,
    wk_in,
    wv_in,
    gain_ref,
    ggain_ref,
    gi_in,
    gb_in,
    ig_ref,
    gwq_ref,
    gwk_ref,
    gwv_ref,
    gwi_ref,
    gwb_ref,
    small_ref,
    q_ref,
    k_ref,
    v_ref,
    xs_ref,
    gm_ref,
    wq_ref,
    wk_ref,
    wv_ref,
    gi_ref,
    gb_ref,
    lowt_ref,
    sum_ref,
    gq_ref,
    gk_ref,
    gv_ref,
    ibuf_ref,
    ibuf2_ref,
    again_ref,
    tabg_ref,
    sm_ref,
    smr_ref,
    bias_ref,
    sums_ref,
    far_ref,
    segk_ref,
    blockof_ref,
    gofeat_ref,
    near_ref,
    acc_ref,
    i0,
    i1,
    i2,
    i3,
    b0,
    b1,
    b2,
    b3,
    a0,
    a1,
    a2,
    a3,
    c0,
    c1,
    c2,
    c3,
    d0,
    d1,
    d2,
    d3,
    s_send,
    s_recv,
    x_send,
    x_recv,
    l_sem,
):
    p = Place(depth)
    length = q_ref.shape[0]
    half_rows = length // 2
    groups = gq_ref.shape[0]
    rest, part = gi_ref.shape[0], gi_ref.shape[-1] // 2
    s_sems, x_sems = (s_send, s_recv), (x_send, x_recv)
    pairs = [(q_in, q_ref), (k_in, k_ref), (v_in, v_ref), (xs_in, xs_ref)]
    pairs += [(gi_in, gi_ref), (gb_in, gb_ref), (gm_in, gm_ref)]
    pairs += [(wq_in, wq_ref), (wk_in, wk_ref), (wv_in, wv_ref)]
    loads = [local(src, dst, l_sem.at[i]) for i, (src, dst) in enumerate(pairs)]
    for one in loads:
        one.start()
    bwd_setup(seg_ref, tabs_ref, bias_ref, sums_ref, far_ref, segk_ref, blockof_ref)
    p.barrier()
    rest_items = []
    for k in range(rest):
        rest_items.append(
            [
                Scatter(
                    p, gi_ref.at[k], part, [r.at[k] for r in (i0, i1, i2, i3)], s_sems, 2 * k, True
                ),
                Scatter(
                    p,
                    gb_ref.at[k],
                    part,
                    [r.at[k] for r in (b0, b1, b2, b3)],
                    s_sems,
                    2 * k + 1,
                    False,
                ),
            ]
        )
    group_items = []
    for j in range(groups):
        group_items.append(
            [
                Scatter(
                    p,
                    ref.at[j],
                    LANES,
                    [r.at[j] for r in bufs],
                    s_sems,
                    2 * rest + 3 * j + i,
                    i != 1,
                )
                for i, (ref, bufs) in enumerate(
                    (
                        (gq_ref, (a0, a1, a2, a3)),
                        (gk_ref, (c0, c1, c2, c3)),
                        (gv_ref, (d0, d1, d2, d3)),
                    )
                )
            ]
        )

    def chunk(k, name):
        if k >= rest:
            return []
        if name == "finish":
            return [
                functools.partial(item.finish, out, k * part)
                for item, out in zip(rest_items[k], (gwi_ref, gwb_ref))
            ]
        return [getattr(item, name) for item in rest_items[k]]

    def group(j, name):
        if name == "finish":
            return [
                functools.partial(item.finish, out, j * LANES)
                for item, out in zip(group_items[j], (gwq_ref, gwk_ref, gwv_ref))
            ]
        return [getattr(item, name) for item in group_items[j]]

    for one in loads[:6]:
        one.wait()
    run_all(chunk(0, "step0"))
    xs = xs_ref.reshape(length, xs_ref.shape[2])
    gain = gain_ref[...]
    low_transposed(xs, gain, lowt_ref)
    run_all(chunk(0, "step1") + chunk(1, "step0"))
    for one in loads[6:]:
        one.wait()

    def group_cols(ref, j):
        return [ref[:, pair_cols(j)], ref[:, pair_cols(j + groups)]]

    def weight_grads(j):
        for target, grad in zip((gq_ref, gk_ref, gv_ref), (q_ref, k_ref, v_ref)):
            both = jnp.concatenate(group_cols(grad, j), 1)
            target[j] = nn(lowt_ref[...], both).astype(BF).reshape(target.shape[1:])

    def group_weights(j):
        pieces = []
        for weight in (wq_ref, wk_ref, wv_ref):
            for at in (j, j + groups):
                pieces.append(flat(weight[:, :, :, :, pair_cols(at)]))
        return jnp.concatenate(pieces, 1)

    def group_sum(rows, j):
        pieces = []
        for grad in (q_ref, k_ref, v_ref):
            for at in (j, j + groups):
                pieces.append(grad[rows, pair_cols(at)])
        return nt(jnp.concatenate(pieces, 1), group_weights(j))

    step = 256
    plan = [
        [],
        chunk(0, "step2") + chunk(1, "step1") + chunk(2, "step0"),
        chunk(0, "step3") + chunk(1, "step2") + chunk(2, "step1"),
        chunk(0, "finish") + chunk(1, "step3") + chunk(2, "step2") + group(0, "step1"),
        chunk(1, "finish") + chunk(2, "step3") + group(0, "step2"),
        chunk(2, "finish") + group(0, "step3") + group(1, "step1"),
    ]

    def one_pair(index, carry):
        at_step(index, plan)
        j, side = lax.div(index, 2), lax.rem(index, 2)
        bwd_pair(
            j + groups * side,
            q_ref,
            k_ref,
            v_ref,
            go_ref,
            ctx_ref,
            feat_ref,
            q_ref,
            k_ref,
            v_ref,
            bias_ref,
            sums_ref,
            far_ref,
            segk_ref,
            blockof_ref,
            gofeat_ref,
            near_ref,
            acc_ref,
        )

        @pl.when(side == 1)
        def _():
            weight_grads(j)
            for i in range(groups):

                @pl.when(j == i)
                def _():
                    run_all(group(i, "step0"))

            for i in range(groups - 1):

                @pl.when(j == i)
                def _():
                    for at in range(length // step):
                        rows = slice(at * step, (at + 1) * step)
                        if i == 0:
                            sum_ref[rows, :] = group_sum(rows, i)
                        else:
                            sum_ref[rows, :] += group_sum(rows, i)

        return carry

    lax.fori_loop(0, 2 * groups, one_pair, 0)
    bwd_table(tabg_ref, sums_ref, far_ref)
    again_ref[...] = jnp.zeros_like(again_ref)
    last = groups - 1

    def finish_rows(own, i):
        half = p.t if own else 1 - p.t
        at = pl.ds(pl.multiple_of(i * step, step), step)
        rows = pl.ds(pl.multiple_of(half * half_rows + i * step, step), step)
        down = sum_ref[rows, :] + group_sum(rows, last)
        inputs = xs_ref[half, at, :].astype(F32)
        scale = rms_scale(inputs)
        normed = inputs * scale
        again_ref[...] += jnp.sum(down * normed, 0, keepdims=True)
        out = gm_ref[rows, :] + rms_back(down, normed, scale, gain)
        if own:
            ig_ref[p.t, at, :] = out
        else:
            ibuf_ref[at, :] = out.astype(BF)

    moves = []
    for i in range(half_rows // step):
        finish_rows(False, i)
        at = pl.ds(i * step, step)
        moves.append(remote(ibuf_ref.at[at], ibuf2_ref.at[at], x_sems, i, p.xpeer))
        moves[-1].start()
    run_all(group(last, "step1") + group(1, "step2") + group(0, "finish"))
    for i in range(half_rows // step):
        finish_rows(True, i)
    model = again_ref.shape[1]
    sm_ref[0, 0:1, :model] = again_ref[...]
    sm_ref[0, 1:2, :model] = ggain_ref[...]
    sm_ref[0, 2:8, :model] = jnp.zeros((6, model), F32)
    sm_ref[0, :, model : model + LANES] = tabg_ref[0:8, :]
    sm_ref[0, :, model + LANES :] = tabg_ref[8:16, :]
    hops = [(p.sib,), (p.ypeer,), (p.xpeer,), tuple(p.zpeers)]
    slot = 0
    beside = [
        group(last, "step2"),
        group(1, "step3"),
        group(last, "step3"),
        group(1, "finish"),
    ]
    for level, peers in enumerate(hops):
        hop = [
            remote(sm_ref.at[level], smr_ref.at[slot + i], x_sems, len(moves) + slot + i, peer)
            for i, peer in enumerate(peers)
        ]
        for one in hop:
            one.start()
        run_all(beside[level])
        total = sm_ref[level]
        for i, one in enumerate(hop):
            one.wait_recv()
            total = total + smr_ref[slot + i]
        slot += len(peers)
        if level + 1 < len(hops):
            sm_ref[level + 1] = total
        else:
            small_ref[...] = total
        for one in hop:
            one.wait_send()
    run_all(group(last, "finish"))
    for i, move in enumerate(moves):
        move.wait_recv()
        at = pl.ds(i * step, step)
        ig_ref[1 - p.t, at, :] = ibuf2_ref[at, :].astype(F32)
        move.wait_send()


def call(kernel, outs, scratch, args, name, collective=None, far=()):
    def spec(array):
        return pl.BlockSpec(memory_space=pl.ANY if array in far else pltpu.VMEM)

    if collective is None:
        params = pltpu.CompilerParams(vmem_limit_bytes=VMEM_BYTES)
    else:
        params = pltpu.CompilerParams(
            vmem_limit_bytes=VMEM_BYTES, collective_id=collective, has_side_effects=True
        )
    return pl.pallas_call(
        kernel,
        out_shape=[jax.ShapeDtypeStruct(shape, dtype) for shape, dtype in outs],
        in_specs=[spec(i) for i in range(len(args))],
        out_specs=[spec(len(args) + i) for i in range(len(outs))],
        scratch_shapes=scratch,
        compiler_params=params,
        name=name,
    )(*args)


def shards(
    inputs,
    segments,
    norm_attn,
    norm_ffn,
    w_query,
    w_key,
    w_value,
    w_out,
    w_in,
    w_back,
    rel_table,
    cotangent,
):
    dp, tensor = lax.axis_size("dp"), lax.axis_size("tensor")
    t = lax.axis_index("tensor")
    rows, width = w_query.shape
    hidden_part = w_in.shape[1]
    model = inputs.shape[2]
    length = segments.shape[2]
    half = inputs.shape[1]
    buckets, heads = rel_table.shape
    depth = dp // 4
    fused = rows % 16 == 0 and dp % 4 == 0 and depth >= 2
    gain_attn, gain_ffn = norm_attn.reshape(1, model), norm_ffn.reshape(1, model)
    table = jnp.pad(rel_table.T, ((0, 8 - heads), (0, LANES - buckets)))
    segment = lax.dynamic_index_in_dim(segments[:, 0], t, 0, False).reshape(length, 1)
    full = (length, model)
    inner = (length, width * tensor)
    square = (depth, 2, 2, rows, 2 * width)
    part = 256
    chunks = hidden_part // part
    pairs = inner[1] // LANES
    dma = pltpu.SemaphoreType.DMA
    halves = (2, half, model)
    fwd_work = [pltpu.VMEM((16, 4 * LANES), F32)] + [pltpu.VMEM((length, LANES), BF)] * 2
    bwd_work = [
        pltpu.VMEM((16, 4 * LANES), F32),
        pltpu.VMEM((16, 4 * LANES), F32),
        pltpu.VMEM((16, LANES), F32),
        pltpu.VMEM((length, LANES), BF),
        pltpu.VMEM((length, LANES), BF),
        pltpu.VMEM((length, LANES), BF),
        pltpu.VMEM((2, LANES, 3 * LANES), F32),
        pltpu.VMEM((length, LANES), F32),
    ]
    ffn_work = [pltpu.VMEM(full, BF), pltpu.VMEM(full[::-1], BF), pltpu.VMEM(full[::-1], BF)]
    rest = [pltpu.VMEM((length, 2 * part), BF)] * 2 + [pltpu.VMEM(full, F32)] * 2
    if fused:
        early = chunks // 2
        here = chunks // 2
        late = chunks - early
        block = (depth, 2, 2, rows, 2 * part)
        xs, coto, tabs, queries, keys, values, ctx, feats, wq, wk, wv, wo, wi, wb = call(
            functools.partial(attend_fused, depth),
            [
                (halves, BF),
                ((half, model), BF),
                ((2, 8, LANES), F32),
                (inner, BF),
                (inner, BF),
                (inner, BF),
                (inner, BF),
                ((pairs, length, LANES), BF),
                (square, BF),
                (square, BF),
                (square, BF),
                (square, BF),
                ((early,) + block, BF),
                ((early,) + block, BF),
            ],
            [pltpu.VMEM(halves, BF), pltpu.VMEM((half, model), F32), pltpu.VMEM((half, model), BF)]
            + [pltpu.VMEM(inner, BF)] * 3
            + [pltpu.VMEM(square, BF)] * 4
            + [pltpu.VMEM((early,) + block, BF)] * 2
            + [pltpu.VMEM(full, BF)]
            + fwd_work
            + [dma((3, 2 * depth + 5))] * 2
            + gather_sems(1 + 2 * early, depth)
            + [dma((3,)), dma((3,)), dma((9 + 2 * early,))],
            (
                inputs,
                cotangent,
                gain_attn,
                table,
                segment,
                w_query,
                w_key,
                w_value,
                w_out,
                w_in,
                w_back,
            ),
            "attention_forward",
            0,
            (1, 11, 14, 15, 16, 19, 20, 21, 22, 23, 24),
        )
        output, grad_middle, grad_context, ggain, gwo, gwi, gwb, gi, gb = call(
            functools.partial(ffn_fused, depth, early, here),
            [
                (halves, F32),
                (full, F32),
                (inner, BF),
                ((1, model), F32),
                ((rows, width), F32),
                ((rows, here * part), F32),
                ((rows, here * part), F32),
                ((chunks - here,) + block, BF),
                ((chunks - here,) + block, BF),
            ],
            [pltpu.VMEM((chunks,) + block, BF)] * 2
            + [pltpu.VMEM(square, BF)]
            + ffn_work
            + [pltpu.VMEM((half, model), F32), pltpu.VMEM(halves, BF)]
            + rest
            + [pltpu.VMEM((half, model), BF)] * 2
            + scatter_bufs(None, depth, rows, width, True)
            + scatter_bufs(here, depth, rows, part, True)
            + scatter_bufs(here, depth, rows, part, False)
            + gather_sems(2 * late, depth)
            + scatter_sems(1 + 2 * here, depth)
            + [dma((1,)), dma((1,)), dma((1 + 2 * chunks,))],
            (xs.reshape(full), ctx, cotangent, coto, gain_ffn, wo, wi, wb, w_in, w_back),
            "feed_forward",
            1,
            (2, 6, 7, 17, 18),
        )
        left = chunks - here
        groups = pairs // 2
        narrow = (groups, depth, 2, 2, rows, 2 * LANES)
        input_grad, gwq, gwk, gwv, gwi_rest, gwb_rest, small = call(
            functools.partial(back_fused, depth),
            [
                (halves, F32),
                ((rows, width), F32),
                ((rows, width), F32),
                ((rows, width), F32),
                ((rows, left * part), F32),
                ((rows, left * part), F32),
                ((8, model + 2 * LANES), F32),
            ],
            [pltpu.VMEM(inner, BF)] * 3
            + [pltpu.VMEM(halves, BF), pltpu.VMEM(full, F32)]
            + [pltpu.VMEM(square, BF)] * 3
            + [pltpu.VMEM((left,) + block, BF)] * 2
            + [pltpu.VMEM(full[::-1], BF), pltpu.VMEM(full, F32)]
            + [pltpu.VMEM(narrow, BF)] * 3
            + [pltpu.VMEM((half, model), BF)] * 2
            + [
                pltpu.VMEM((1, model), F32),
                pltpu.VMEM((16, LANES), F32),
                pltpu.VMEM((4, 8, model + 2 * LANES), F32),
                pltpu.VMEM((depth + 2, 8, model + 2 * LANES), F32),
            ]
            + bwd_work
            + scatter_bufs(left, depth, rows, part, True)
            + scatter_bufs(left, depth, rows, part, False)
            + scatter_bufs(groups, depth, rows, LANES, True)
            + scatter_bufs(groups, depth, rows, LANES, False)
            + scatter_bufs(groups, depth, rows, LANES, True)
            + scatter_sems(2 * left + 3 * groups, depth)
            + [dma((depth + 4,)), dma((depth + 4,)), dma((10,))],
            (
                queries,
                keys,
                values,
                grad_context,
                ctx,
                feats,
                segment,
                tabs,
                xs,
                grad_middle,
                wq,
                wk,
                wv,
                gain_attn,
                ggain,
                gi,
                gb,
            ),
            "attention_backward",
            2,
            (0, 1, 2, 8, 9, 10, 11, 12, 15, 16),
        )
        gwi = jnp.concatenate([gwi, gwi_rest], 1)
        gwb = jnp.concatenate([gwb, gwb_rest], 1)
        gain_attn_grad, gain_ffn_grad = small[0, :model], small[1, :model]
        tables = jnp.stack([small[:, model : model + LANES], small[:, model + LANES :]])
    else:

        def whole(weight):
            weight = lax.all_gather(weight, "dp", axis=0, tiled=True)
            return lax.all_gather(weight, "tensor", axis=1, tiled=True)

        def exchanged(local_part):
            own = lax.dynamic_index_in_dim(local_part, t, 0, False)
            other = lax.dynamic_index_in_dim(local_part, 1 - t, 0, False)
            other = lax.ppermute(other, "tensor", [(0, 1), (1, 0)])
            first = jnp.where(t == 0, own, other)
            second = jnp.where(t == 0, other, own)
            return jnp.concatenate([first, second], 0)

        def returned(seq):
            mine = lax.dynamic_slice_in_dim(seq, t * half, half, 0)
            other = lax.dynamic_slice_in_dim(seq, (1 - t) * half, half, 0)
            other = lax.ppermute(other, "tensor", [(0, 1), (1, 0)])
            return jnp.stack([jnp.where(t == 0, mine, other), jnp.where(t == 0, other, mine)])

        def scattered(grad):
            grad = lax.psum_scatter(grad.astype(F32), "tensor", scatter_dimension=1, tiled=True)
            return lax.psum_scatter(grad, "dp", scatter_dimension=0, tiled=True)

        xs = exchanged(inputs)
        tabs = lax.all_gather(table, "tensor", axis=0)
        wq, wk, wv, wo, wi, wb = (
            whole(w) for w in (w_query, w_key, w_value, w_out, w_in, w_back)
        )
        queries, keys, values = call(
            k1_plain,
            [(inner, BF)] * 3,
            [pltpu.VMEM(full, BF)],
            (xs, gain_attn, wq, wk, wv),
            "project",
        )
        ctx, feats = call(
            fwd_kernel,
            [(inner, BF), ((pairs, length, LANES), BF)],
            fwd_work,
            (queries, keys, values, segment, tabs),
            "attention_forward",
        )
        out_seq, grad_middle, grad_context, ggain, gwo, gwi, gwb = call(
            k3_plain,
            [
                (full, F32),
                (full, F32),
                (inner, BF),
                ((1, model), F32),
                (wo.shape, BF),
                (wi.shape, BF),
                (wb.shape, BF),
            ],
            ffn_work + [pltpu.VMEM(full, BF)] + rest,
            (xs, ctx, exchanged(cotangent), gain_ffn, wo, wi, wb),
            "feed_forward",
        )
        output = returned(out_seq)
        gwo, gwi, gwb = scattered(gwo), scattered(gwi), scattered(gwb)
        dq, dk, dv, table_grad = call(
            bwd_kernel,
            [(inner, BF), (inner, BF), (inner, BF), ((16, LANES), F32)],
            bwd_work,
            (queries, keys, values, grad_context, ctx, feats, segment, tabs),
            "attention_backward",
        )
        ig_seq, gwq, gwk, gwv, again = call(
            k5_plain,
            [(full, F32), (wq.shape, BF), (wk.shape, BF), (wv.shape, BF), ((1, model), F32)],
            [pltpu.VMEM((model, length), BF)],
            (xs, grad_middle, dq, dk, dv, wq, wk, wv, gain_attn),
            "projection_gradients",
        )
        input_grad = returned(ig_seq)
        gwq, gwk, gwv = scattered(gwq), scattered(gwk), scattered(gwv)
        again, ggain, tables = lax.psum((again, ggain, table_grad), ("dp", "tensor"))
        gain_attn_grad, gain_ffn_grad = again[0], ggain[0]
        tables = tables.reshape(2, 8, LANES)
    table_out = lax.dynamic_index_in_dim(tables, t, 0, False)[:heads, :buckets].T
    return (
        output,
        input_grad,
        gain_attn_grad,
        gain_ffn_grad,
        gwq,
        gwk,
        gwv,
        gwo,
        gwi,
        gwb,
        table_out,
    )


def solution(mesh):
    weight = P("dp", "tensor")
    tokens = P(None, ("dp", "tensor"), None)
    return jax.shard_map(
        shards,
        mesh=mesh,
        in_specs=(
            tokens,
            P(None, "dp", None),
            P(),
            P(),
            weight,
            weight,
            weight,
            weight,
            weight,
            weight,
            P(None, "tensor"),
            tokens,
        ),
        out_specs=(
            tokens,
            tokens,
            P(),
            P(),
            weight,
            weight,
            weight,
            weight,
            weight,
            weight,
            P(None, "tensor"),
        ),
        check_vma=False,
    )
```

time: 340 us -> 300 us (0.88)
  Pallas kernels: 322 us -> 281 us
    pallas_call x5 -> x3, Pallas kernels: 322 us -> 281 us  [call(): pl.pallas_call(kernel, out_shape=[jax.ShapeDtypeStruct(shape, dtype) for...]
    unnamed x24 -> x22, local copies, waits for them, and re-layouts: 9.57 us -> 8.14 us
where the time goes in v2:
time: 300 us; the launch traced here: 299 us
  Pallas kernels  281 us (94%)
  local copies, waits for them, and re-layouts  15.7 us (5%)
    pallas_call x3, Pallas kernels, call(): pl.pallas_call(kernel, out_shape=[jax.ShapeDtypeStruct(shape, dtype) for...  281 us
    unnamed x22, local copies, waits for them, and re-layouts  8.14 us

profile of v2, /device:TPU:0, one launch (start us, length us, event | category | flops | bytes accessed | tf_op | source)
XLA Modules:
  0.0 299.2 jit_solution(3902072197133215453)
XLA Ops:
  0.6 0.0 copy-start
  0.7 1.3 reshape.37.gain_ref
  1.9 1.3 reshape.40.gain_ref
  3.2 0.0 copy-done
  3.2 1.3 pad.4.tab_ref
  4.5 1.0 copy.23.seg_ref
  5.5 85.4 %attention_forward.1 = (bf16[2,512,768]{2,1,0:T(8,128)(2,1)}, bf16[512,768]{1,0:T(8,128)(2,1)}, f32[2,8,128]{2,1,0:T(8,128)}, bf16[1024,768]{1,0:T(8,128)(2,1)},...) custom-call(bf16[2,512,768]{2,1,0:T(8,128)(2,1)} %x_ref.1, ...), custom_call_target="tpu_custom_call" | custom-call | tf_op jit(solution)/shard_map/attention_forward/pallas_call | solution.py:1611
  90.9 102.4 %feed_forward.1 = (f32[2,512,768]{2,1,0:T(8,128)}, f32[1024,768]{1,0:T(8,128)}, bf16[1024,768]{1,0:T(8,128)(2,1)}, f32[1,768]{1,0:T(1,128)}, f32[48,384]{1,0:T(8...) custom-call(bf16[1024,768]{1,0:T(8,128)(2,1)} %bitcast.12, ...), custom_call_target="tpu_custom_call" | custom-call | tf_op jit(solution)/shard_map/feed_forward/pallas_call | solution.py:1611
  193.3 0.0 copy-start.2
  193.3 0.0 copy-start.3
  193.3 93.1 %attention_backward.1 = (f32[2,512,768]{2,1,0:T(8,128)}, f32[48,384]{1,0:T(8,128)}, f32[48,384]{1,0:T(8,128)}, f32[48,384]{1,0:T(8,128)}, f32[48,768]{1,0:T(8,12...) custom-call(bf16[1024,768]{1,0:T(8,128)(2,1)} %get-tuple-element.48.q_in, bf16[1024,768]{1,0:T(8,128)(2,1)} %get-tuple-element.49.k_in, ...), custom_call_target="tpu_custom_call" | custom-call | tf_op jit(solution)/shard_map/attention_backward/pallas_call | solution.py:1611
  286.5 1.4 slice_reduce_fusion
  287.9 0.7 slice_bitcast_fusion.1
  288.6 0.6 slice_bitcast_fusion
  289.2 0.0 copy-done.2
  289.2 0.0 copy-done.3
  289.2 1.8 pad_maximum_fusion
  291.0 0.0 copy-start.1
  291.0 3.9 %copy.31 = f32[2,512,768]{2,1,0:T(8,128)} copy(f32[2,512,768]{2,1,0:T(8,128)} %get-tuple-element.88) | data formatting | bytes 6291456
  294.9 0.0 copy-done.1
  294.9 0.0 copy-start.7
  294.9 0.0 copy-start.6
  294.9 0.0 copy-start.5
  294.9 0.0 copy-start.4
  294.9 1.7 copy.32
  296.6 0.0 copy-done.7
  296.6 0.6 copy.33
  297.3 0.0 copy-done.6
  297.3 0.6 copy.34
  297.9 0.0 copy-done.5
  297.9 0.6 copy.35
  298.5 0.0 copy-done.4
  298.5 0.6 copy.36
  (2 shorter events, 0.0 us)
Async XLA Ops:
  0.6 2.6 copy-start
  193.3 95.9 %copy-start.2 = (f32[48,768]{1,0:T(8,128)S(1)}, f32[48,768]{1,0:T(8,128)}, u32[]{:S(2)}) copy-start(f32[48,768]{1,0:T(8,128)} %get-tuple-element.67) | copy-start | bytes 442372
  193.3 95.9 %copy-start.3 = (f32[48,768]{1,0:T(8,128)S(1)}, f32[48,768]{1,0:T(8,128)}, u32[]{:S(2)}) copy-start(f32[48,768]{1,0:T(8,128)} %get-tuple-element.69) | copy-start | bytes 442372
  291.0 3.9 %copy-start.1 = (f32[2,512,768]{2,1,0:T(8,128)S(1)}, f32[2,512,768]{2,1,0:T(8,128)}, u32[]{:S(2)}) copy-start(f32[2,512,768]{2,1,0:T(8,128)} %get-tuple-element.89) | copy-start | bytes 9437188
  294.9 1.7 copy-start.7
  294.9 2.3 copy-start.6
  294.9 3.0 copy-start.5
  294.9 3.6 %copy-start.4 = (f32[48,384]{1,0:T(8,128)S(1)}, f32[48,384]{1,0:T(8,128)}, u32[]{:S(2)}) copy-start(f32[48,384]{1,0:T(8,128)} %get-tuple-element.95) | copy-start | bytes 221188
